TPU v7x, 256 devices: a whole 4x4x8 slice. The times are simulated.
256 devices in a mesh: gx: 32 (over z, x), gy: 8 (over y, core).
Axes of the slice: x: 4, y: 4, z: 8, core: 2. Of those that a mesh axis runs over, the one named last changes fastest.
Arguments:
- newton_residual: float32 [16, 512, 2048], P(None, 'gx', 'gy'), may hold values from -6 to 6
- pressure_head: float32 [16, 512, 2048], P(None, 'gx', 'gy'), may hold values from -6 to 1
- conductivity: float32 [16, 512, 2048], P(None, 'gx', 'gy'), may hold values from 0.1 to 10
- land_use: int32 [512, 2048], P('gx', 'gy'), may hold values from 0 to 7
- storage_table: float32 [8], replicated, may hold values from 0.002 to 0.05
- return_table: float32 [8], replicated, may hold values from 0.2 to 0.9
- well_cells: int32 [32, 8, 32], P('gx', 'gy'), may hold values from 0 to 65535
- well_rates: float32 [32, 8, 32], P('gx', 'gy'), may hold values from 0.5 to 4
- return_cells: int32 [32, 8, 32], P('gx', 'gy'), may hold values from 0 to 4095
Outputs:
- correction: float32 [16, 512, 2048], P(None, 'gx', 'gy')
Inputs may be any that keep to these rules, and one draw needn't show every extreme that they name: `well_cells`: A well's cell index z * 16 * 256 + x * 256 + y addresses layer z, column x, y of its tile; wells may share a cell. `return_cells`: index x * 256 + y of a column of the well's tile.
All inputs are finite; a program needn't handle non-finite values.
Results may differ from a plain program's by a relative error of at most 0.0001.
Values sent between devices are 32-bit elements; how exact they have to be, the bound alone decides.
A program may use at most 128 MiB of HBM per device.

v0:
```python
import functools

import jax
import jax.numpy as jnp
from jax import lax
from jax.experimental import pallas as pl
from jax.experimental.pallas import tpu as pltpu
from jax.sharding import PartitionSpec as P

NZ = 16
CLASSES = 8
COARSE_SWEEPS = 12
OMEGA = 0.8
VERTICAL = 4.0
ALPHA = 0.5
F32 = jnp.float32
MESH = pl.DeviceIdType.MESH

NX = (16, 8, 4, 2)
NY = (256, 128, 64, 32)
XR = (24, 16, 8, 8)
YR = (384, 256, 128, 128)
OWN_R = (16, 8, 8, 8)
OWN_W = (256, 128, 128, 128)
EOFF = (0, 0, 4, 2)
NOFF = (0, 0, 64, 32)

THREE = ((3, 0), (2, 3), (2, 5))
FOUR = ((2, 0), (2, 2), (2, 4), (2, 6))
ONE = ((2, 0),)
EXCHANGES = {
    "e0": (0, 8, THREE),
    "c1": (1, 8, FOUR),
    "c2": (2, 8, FOUR),
    "c3": (3, 8, FOUR),
    "x1": (1, 2, ONE),
    "x2": (2, 2, ONE),
    "x3": (3, 2, ONE),
    "u3": (3, 2, ONE),
    "u2": (2, 2, ONE),
    "u1": (1, 2, ONE),
    "u0": (0, 2, ONE),
}
GY, GX = 8, 32
N_HALO = 8 * len(EXCHANGES)
N_SEM = N_HALO + 2 * (GY - 1) + 2 * (GX - 1)
LEVEL_ARRAYS = ("E", "N", "D", "diag", "g", "inv", "rhs", "u", "f")


def rot(value, shift, axis):
    shift %= value.shape[axis]
    return value if shift == 0 else pltpu.roll(value, shift, axis)


def iota(shape, axis):
    return lax.broadcasted_iota(jnp.int32, shape, axis)


def between(index, start, count):
    return (index >= start) & (index < start + count)


def exact_dot(left, right):
    return jnp.dot(left, right, precision=lax.Precision.HIGHEST, preferred_element_type=F32)


def scratch_plan():
    plan = {}
    for level in range(4):
        for name in LEVEL_ARRAYS:
            plan[f"{name}{level}"] = pltpu.VMEM((NZ, XR[level], YR[level]), F32)
    plan["P0"] = pltpu.VMEM((NZ, XR[0], YR[0]), F32)
    plan["S0"] = pltpu.VMEM((NZ, XR[0], YR[0]), F32)
    for name in ("E4", "N4", "g4", "inv4", "rhs4", "u4", "f4"):
        plan[name] = pltpu.VMEM((NZ * 16, 128), F32)
    for name in ("ta", "tb", "tc", "td"):
        plan[name] = pltpu.VMEM((NZ, 2, 16, 128), F32)
    for name, (level, group, _) in EXCHANGES.items():
        tiles = NZ * group // 8
        for kind in ("s", "r"):
            plan[f"{name}_{kind}x"] = pltpu.VMEM((2, tiles, 8, OWN_W[level]), F32)
            plan[f"{name}_{kind}y"] = pltpu.VMEM((2, OWN_R[level], 128), F32)
        plan[f"{name}_rc"] = pltpu.VMEM((4, 8, 128), F32)
    for name, count in (("gc", 4), ("gr", 1)):
        plan[f"{name}_s1"] = pltpu.VMEM((count, 8, 128), F32)
        plan[f"{name}_r1"] = pltpu.VMEM((GY, count, 8, 128), F32)
        plan[f"{name}_s2"] = pltpu.VMEM((count, 8, 128), F32)
        plan[f"{name}_r2"] = pltpu.VMEM((count, GX * 8, 128), F32)
    plan["send"] = pltpu.SemaphoreType.DMA((N_SEM,))
    plan["recv"] = pltpu.SemaphoreType.DMA((N_SEM,))
    return plan


PLAN = scratch_plan()


def kernel(
    residual, pressure, conductivity, land_use, storage_table, return_table,
    well_cells, well_rates, return_cells, out, *scratch,
):
    ref = dict(zip(PLAN, scratch))
    gx = lax.axis_index("gx")
    gy = lax.axis_index("gy")

    def device(dx, dy):
        return (lax.rem(gx + (dx + GX), GX), lax.rem(gy + (dy + GY), GY))

    peers = [(dx, dy) for dx in (-1, 1) for dy in (-1, 1)]
    peers += [(0, d) for d in range(1, GY)] + [(d, 0) for d in range(1, GX)]
    barrier = pltpu.get_barrier_semaphore()
    for dx, dy in peers:
        pl.semaphore_signal(barrier, inc=1, device_id=device(dx, dy), device_id_type=MESH)

    started = []

    def remote(src, dst, index, dx, dy):
        copy = pltpu.make_async_remote_copy(
            src_ref=src, dst_ref=dst, send_sem=ref["send"].at[index], recv_sem=ref["recv"].at[index],
            device_id=device(dx, dy), device_id_type=MESH,
        )
        copy.start()
        started.append(copy)
        return copy

    def pack(name, get):
        level, group, items = EXCHANGES[name]
        nx, ny, rows, width = NX[level], NY[level], OWN_R[level], OWN_W[level]
        row8 = iota((8, width), 0)
        lane = iota((rows, 128), 1)
        y_lo = jnp.zeros((rows, 128), F32)
        y_hi = jnp.zeros((rows, 128), F32)
        per_tile = 8 // group
        for z in range(NZ):
            if z % per_tile == 0:
                x_lo = jnp.zeros((8, width), F32)
                x_hi = jnp.zeros((8, width), F32)
            slot = z % per_tile
            for k, (w, o) in enumerate(items):
                value = get(k, z)
                lo = group * slot + o
                hi = group * (slot + 1) - o
                x_lo = jnp.where(between(row8, lo, w), rot(value[0:8], lo, 0), x_lo)
                x_hi = jnp.where(
                    between(row8, (8 - w + hi) % 8, w), rot(value[rows - 8 : rows], 8 - nx + hi, 0), x_hi
                )
                lo = group * z + o
                hi = group * (z + 1) - o
                y_lo = jnp.where(between(lane, lo, w), rot(value[:, 0:128], lo, 1), y_lo)
                y_hi = jnp.where(
                    between(lane, (128 - w + hi) % 128, w),
                    rot(value[:, width - 128 : width], 128 - ny + hi, 1),
                    y_hi,
                )
            if slot == per_tile - 1:
                ref[f"{name}_sx"][0, z // per_tile] = x_lo
                ref[f"{name}_sx"][1, z // per_tile] = x_hi
        ref[f"{name}_sy"][0] = y_lo
        ref[f"{name}_sy"][1] = y_hi

    def send(name):
        level = EXCHANGES[name][0]
        rows = OWN_R[level]
        base = 8 * list(EXCHANGES).index(name)
        sx, sy = ref[f"{name}_sx"], ref[f"{name}_sy"]
        rx, ry, rc = ref[f"{name}_rx"], ref[f"{name}_ry"], ref[f"{name}_rc"]
        first, last = pl.ds(0, 8), pl.ds(rows - 8, 8)
        moves = (
            (sx.at[0], rx.at[0], -1, 0),
            (sx.at[1], rx.at[1], 1, 0),
            (sy.at[0], ry.at[0], 0, -1),
            (sy.at[1], ry.at[1], 0, 1),
            (sy.at[0, first], rc.at[0], -1, -1),
            (sy.at[0, last], rc.at[1], 1, -1),
            (sy.at[1, first], rc.at[2], -1, 1),
            (sy.at[1, last], rc.at[3], 1, 1),
        )
        return [remote(src, dst, base + i, dx, dy) for i, (src, dst, dx, dy) in enumerate(moves)]

    def unpack(name, copies, targets, fills, masked=None):
        level, group, items = EXCHANGES[name]
        nx, ny, rows, width = NX[level], NY[level], OWN_R[level], OWN_W[level]
        eoff, noff = EOFF[level], NOFF[level]
        for copy in copies:
            copy.wait_recv()
        rx, ry, rc = ref[f"{name}_rx"], ref[f"{name}_ry"], ref[f"{name}_rc"]
        row8 = iota((8, 128), 0)
        strips = []
        for side in (0, 1):
            east, west = rc[2 * side], rc[2 * side + 1]
            if level <= 1:
                strips.append(jnp.concatenate([ry[side], jnp.where(row8 < 4, east, west)], axis=0))
            else:
                strips.append(
                    jnp.where(
                        row8 < nx, ry[side],
                        jnp.where(row8 < nx + 2, rot(east, eoff, 0), rot(west, 8 - nx, 0)),
                    )
                )
        strip_n, strip_s = strips
        rows_all = XR[level]
        lane = iota((rows_all, 128), 1)
        row = iota((8, width), 0)
        per_tile = 8 // group
        for z in range(NZ):
            tile, slot = z // per_tile, z % per_tile
            for k, (w, o) in enumerate(items):
                target, fill = targets[k], fills[k]
                from_e = rot(rx[0, tile], eoff - (group * slot + o), 0)
                from_w = rot(rx[1, tile], o - group * (slot + 1), 0)
                from_n = rot(strip_n, noff - (group * z + o), 1)
                from_s = rot(strip_s, o - group * (z + 1), 1)
                if masked is not None and k == 0:
                    from_e, from_w = from_e * masked[0], from_w * masked[1]
                    from_n, from_s = from_n * masked[2], from_s * masked[3]
                in_e, in_w = between(row, eoff, w), row >= 8 - w
                in_n, in_s = between(lane, noff, w), lane >= 128 - w
                if level <= 1:
                    target[z, rows : rows + 8, 0:width] = jnp.where(in_e, from_e, jnp.where(in_w, from_w, fill))
                    target[z, :, width : width + 128] = jnp.where(in_n, from_n, jnp.where(in_s, from_s, fill))
                else:
                    value = jnp.where(in_e, from_e, jnp.where(in_w, from_w, target[z]))
                    target[z] = jnp.where(in_n, from_n, jnp.where(in_s, from_s, value))

    def factor(level):
        diag, down, g, inv = (ref[f"{name}{level}"] for name in ("diag", "D", "g", "inv"))
        before = None
        for z in range(NZ):
            pivot = diag[z]
            if z > 0:
                pivot = pivot - before * down[z - 1]
            inverse = 1.0 / pivot
            inv[z] = inverse
            if z < NZ - 1:
                before = down[z] * inverse
                g[z] = before

    def back_substitute(level, update):
        g, inv, f = (ref[f"{name}{level}"] for name in ("g", "inv", "f"))
        value = f[NZ - 1] * inv[NZ - 1]
        update(NZ - 1, value)
        for z in range(NZ - 2, -1, -1):
            value = f[z] * inv[z] + g[z] * value
            update(z, value)

    def first_sweep(level):
        g, f, rhs, u = (ref[f"{name}{level}"] for name in ("g", "f", "rhs", "u"))
        value = rhs[0]
        f[0] = value
        for z in range(1, NZ):
            value = rhs[z] + g[z - 1] * value
            f[z] = value

        def update(z, solved):
            u[z] = OMEGA * solved

        back_substitute(level, update)

    def lateral(level, z, u):
        east, north = ref[f"E{level}"][z], ref[f"N{level}"][z]
        return (
            east * rot(u, -1, 0) + rot(east * u, 1, 0) + north * rot(u, -1, 1) + rot(north * u, 1, 1)
        )

    def sweep(level):
        g, f, rhs, u = (ref[f"{name}{level}"] for name in ("g", "f", "rhs", "u"))
        value = None
        for z in range(NZ):
            right = rhs[z] + lateral(level, z, u[z])
            value = right if z == 0 else right + g[z - 1] * value
            f[z] = value

        def update(z, solved):
            old = u[z]
            u[z] = old + OMEGA * (solved - old)

        back_substitute(level, update)

    def remainder(level, z):
        diag, down, rhs, u = (ref[f"{name}{level}"] for name in ("diag", "D", "rhs", "u"))
        here = u[z]
        value = rhs[z] + lateral(level, z, here) - diag[z] * here
        if z < NZ - 1:
            value = value + down[z] * u[z + 1]
        if z > 0:
            value = value + down[z - 1] * u[z - 1]
        return value[0 : OWN_R[level], 0 : OWN_W[level]]

    def tiles_of(level):
        return OWN_W[level] // 128

    def put_rows(buffer, level, z, value):
        for t in range(tiles_of(level)):
            buffer[z, t, 0 : OWN_R[level], :] = value[:, 128 * t : 128 * (t + 1)]

    def row_half(buffer, level, z, odd):
        return jnp.concatenate(
            [buffer[z, t, pl.ds(odd, 8, stride=2), :] for t in range(tiles_of(level))], axis=1
        )

    def lane_matrix(level, kind):
        fine = iota((OWN_W[level], 128), 0)
        coarse = iota((OWN_W[level], 128), 1)
        half = NY[level] // 2
        if kind == "sum":
            hit = between(fine - 2 * coarse, 0, 2)
        else:
            hit = fine == 2 * coarse + (1 if kind == "odd" else 0)
        return jnp.where(hit & (coarse < half), 1.0, 0.0).astype(F32)

    def keep_own(level, value, fill):
        if level == 1:
            return value
        own = (iota((8, 128), 0) < (NX[level] if level < 4 else 1)) & (
            iota((8, 128), 1) < (NY[level] if level < 4 else 16)
        )
        return jnp.where(own, value, fill)

    def clear_low_rows(buffer):
        for z in range(NZ):
            for t in range(2):
                buffer[z, t, 8:16, :] = jnp.zeros((8, 128), F32)

    def restrict(level):
        for z in range(NZ):
            put_rows(ref["ta"], level, z, remainder(level, z))
        summed = jnp.concatenate(
            [row_half(ref["ta"], level, z, 0) + row_half(ref["ta"], level, z, 1) for z in range(NZ)], axis=0
        )
        coarse = exact_dot(summed, lane_matrix(level, "sum"))
        return [keep_own(level + 1, coarse[8 * z : 8 * z + 8], 0.0) for z in range(NZ)]

    def coarsen(level):
        names = ("E", "N", "D", "diag")
        buffers = [ref[name] for name in ("ta", "tb", "tc", "td")]
        for z in range(NZ):
            for name, buffer in zip(names, buffers):
                put_rows(buffer, level, z, ref[f"{name}{level}"][z, 0 : OWN_R[level], 0 : OWN_W[level]])
        odd_e, sum_n, sum_d, sum_g = [], [], [], []
        for z in range(NZ):
            e0, e1 = (row_half(buffers[0], level, z, odd) for odd in (0, 1))
            n0, n1 = (row_half(buffers[1], level, z, odd) for odd in (0, 1))
            d0, d1 = (row_half(buffers[2], level, z, odd) for odd in (0, 1))
            g0, g1 = (row_half(buffers[3], level, z, odd) for odd in (0, 1))
            odd_e.append(e1)
            sum_n.append(n0 + n1)
            sum_d.append(d0 + d1)
            sum_g.append(g0 + g1 - 2.0 * e0)
        total = lane_matrix(level, "sum")
        count = NZ * 8
        summed = exact_dot(jnp.concatenate(odd_e + sum_d + sum_g, axis=0), total)
        north = jnp.concatenate(sum_n, axis=0)
        north_odd = exact_dot(north, lane_matrix(level, "odd"))
        north_even = exact_dot(north, lane_matrix(level, "even"))
        result = []
        for z in range(NZ):
            at = slice(8 * z, 8 * z + 8)
            result.append(
                (
                    keep_own(level + 1, summed[8 * z : 8 * z + 8], 0.0),
                    keep_own(level + 1, north_odd[at], 0.0),
                    keep_own(level + 1, summed[count + 8 * z : count + 8 * z + 8], 0.0),
                    keep_own(
                        level + 1,
                        summed[2 * count + 8 * z : 2 * count + 8 * z + 8] - 2.0 * north_even[at],
                        1.0,
                    ),
                )
            )
        return result

    def store_coarse(level, values):
        for z in range(NZ):
            for name, value in zip(("E", "N", "D", "diag"), values[z]):
                ref[f"{name}{level}"][z, 0:8, 0:128] = value

    def prolong(level):
        coarse = jnp.concatenate([ref[f"u{level + 1}"][z, 0:8, 0:128] for z in range(NZ)], axis=0)
        from_lane = iota((128, OWN_W[level]), 0)
        to_lane = iota((128, OWN_W[level]), 1)
        hit = between(to_lane - 2 * from_lane, 0, 2) & (to_lane < NY[level])
        fine = exact_dot(coarse, jnp.where(hit, 1.0, 0.0).astype(F32))
        buffer = ref["ta"]
        u = ref[f"u{level}"]
        rows, width = OWN_R[level], OWN_W[level]
        for z in range(NZ):
            for t in range(tiles_of(level)):
                piece = fine[8 * z : 8 * z + 8, 128 * t : 128 * (t + 1)]
                buffer[z, t, pl.ds(0, 8, stride=2), :] = piece
                buffer[z, t, pl.ds(1, 8, stride=2), :] = piece
        for z in range(NZ):
            add = jnp.concatenate([buffer[z, t, 0:rows, :] for t in range(tiles_of(level))], axis=1)
            u[z, 0:rows, 0:width] = u[z, 0:rows, 0:width] + add

    lane8 = iota((8, 128), 1)
    row8 = iota((8, 128), 0)
    at_sum = (lane8 == 48) & (row8 == 0)

    def pack_tile(values):
        row16 = iota((16, 128), 0)
        lane16 = iota((16, 128), 1)
        stacked = jnp.zeros((16, 128), F32)
        for z in range(NZ):
            stacked = jnp.where(row16 == z, jnp.broadcast_to(values[z][0:1], (16, 128)), stacked)
        stacked = jnp.where(lane16 < 16, stacked, 0.0)
        return rot(stacked[0:8], 16, 1) + rot(stacked[8:16], 80, 1)

    def total_of(value):
        return jnp.sum(jnp.sum(value, axis=1, keepdims=True), axis=0, keepdims=True)

    def gather_columns(name, tiles, part, base):
        for a, tile in enumerate(tiles):
            ref[f"{name}_s1"][a] = jnp.where(at_sum, part, tile) if a == 0 else tile
        return [
            remote(ref[f"{name}_s1"], ref[f"{name}_r1"].at[d], base + d - 1, 0, d) for d in range(1, GY)
        ]

    def gather_rows(name, copies, base):
        for copy in copies:
            copy.wait_recv()
        s1, r1, s2, r2 = (ref[f"{name}_{kind}"] for kind in ("s1", "r1", "s2", "r2"))
        for a in range(s1.shape[0]):
            tiles = [s1[a]] + [r1[d, a] for d in range(1, GY)]
            clean = [jnp.where(at_sum, 0.0, tiles[i]) if a == 0 else tiles[i] for i in (0, 1, GY - 1)]
            window = clean[0] + rot(clean[1], -16, 1) + rot(clean[2], 16, 1)
            if a == 0:
                parts = tiles[0]
                for tile in tiles[1:]:
                    parts = parts + tile
                window = jnp.where(at_sum, parts, window)
            s2[a] = window
            r2[a, 0:8, :] = window
        return [
            remote(s2, r2.at[:, pl.ds(8 * (GX - d), 8), :], base + d - 1, d, 0) for d in range(1, GX)
        ]

    def coarse_layer(buffer, a, z):
        sub, half = z % 8, z // 8
        pieces = [buffer[a, pl.ds(64 * i + sub, 8, stride=8), :] for i in range(4)]
        low = jnp.concatenate(pieces[0:2], axis=0)
        high = jnp.concatenate(pieces[2:4], axis=0)
        lane = iota((16, 128), 1)
        if half == 0:
            return jnp.where(lane < 64, low, rot(high, 64, 1))
        return jnp.where(lane < 64, rot(low, 64, 1), high)

    def coarse_sum(buffer):
        value = jnp.where(at_sum, buffer[0, 0:8, :], 0.0)
        for k in range(1, GX):
            value = value + jnp.where(at_sum, buffer[0, 8 * k : 8 * k + 8, :], 0.0)
        return total_of(value)

    def coarse_at(name, z):
        return ref[name][16 * z : 16 * z + 16, :]

    clear_low_rows(ref["ta"])
    clear_low_rows(ref["tb"])
    clear_low_rows(ref["tc"])
    clear_low_rows(ref["td"])
    use = land_use[...]
    table = jnp.zeros(use.shape, F32)
    fraction = jnp.zeros(use.shape, F32)
    for category in range(CLASSES):
        table = table + jnp.where(use == category, storage_table[category], 0.0)
        fraction = fraction + jnp.where(use == category, return_table[category], 0.0)
    cells, rates, returns = well_cells[...], well_rates[...], return_cells[...]
    wells = rates.shape[1]

    def hits(count, index):
        return iota((count, wells), 0) == index

    def outer(count, index_row, index_column):
        left = jnp.where(hits(count, index_row), rates, 0.0)
        right = jnp.where(hits(256, index_column), 1.0, 0.0).astype(F32)
        return lax.dot_general(
            left, right, (((1,), (1,)), ((), ())),
            precision=lax.Precision.HIGHEST, preferred_element_type=F32,
        )

    pumped = outer(256, cells >> 8, cells & 255)
    recharge = fraction * outer(16, returns >> 8, returns & 255)
    storage_sum = jnp.zeros((16, 256), F32)
    for z in range(NZ):
        relief = jnp.exp(ALPHA * jnp.minimum(pressure[z], 0.0))
        ref["P0"][z, 0:16, 0:256] = conductivity[z] * relief
        storage = table * relief
        ref["S0"][z, 0:16, 0:256] = storage
        storage_sum = storage_sum + storage
        source = residual[z] - pumped[16 * z : 16 * z + 16]
        if z == 0:
            source = source + recharge
        ref["rhs0"][z, 0:16, 0:256] = source
    first = [ref["P0"], ref["S0"], ref["rhs0"]]
    pack("e0", lambda k, z: first[k][z, 0:16, 0:256])
    pl.semaphore_wait(barrier, len(peers))
    copies = send("e0")

    flags = [
        jnp.where(inside, 1.0, 0.0).astype(F32)
        for inside in (gx < GX - 1, gx > 0, gy < GY - 1, gy > 0)
    ]
    row24 = iota((24, 128), 0)
    by_row = jnp.where(row24 < 16, 1.0, jnp.where(row24 < 20, flags[0], flags[1]))
    unpack("e0", copies, first, (0.0, 1.0, 0.0), (flags[0], flags[1], by_row * flags[2], by_row * flags[3]))

    def harmonic(first_value, second_value):
        return 2.0 * first_value * second_value / (first_value + second_value + 1e-30)

    above = None
    for z in range(NZ):
        here = ref["P0"][z]
        east = harmonic(here, rot(here, -1, 0))
        north = harmonic(here, rot(here, -1, 1))
        diagonal = ref["S0"][z] + east + rot(east, 1, 0) + north + rot(north, 1, 1)
        if z > 0:
            diagonal = diagonal + above
        if z < NZ - 1:
            above = VERTICAL * harmonic(here, ref["P0"][z + 1])
            diagonal = diagonal + above
        else:
            above = jnp.zeros_like(here)
        ref["D0"][z] = above
        ref["E0"][z] = east
        ref["N0"][z] = north
        ref["diag0"][z] = diagonal
    factor(0)

    arrays = {level: [ref[f"{name}{level}"] for name in ("E", "N", "D", "diag")] for level in (1, 2, 3)}
    fills = (0.0, 0.0, 0.0, 1.0)
    sent = {}

    def own_coefficients(level):
        store_coarse(level, coarsen(level - 1))
        pack(f"c{level}", lambda k, z: arrays[level][k][z, 0:8, 0:128])
        sent[level] = send(f"c{level}")

    own_coefficients(1)

    def down(level):
        first_sweep(level)
        sweep(level)
        values = restrict(level)
        if level < 3:
            for z in range(NZ):
                ref[f"rhs{level + 1}"][z, 0:8, 0:128] = values[z]
            pack(f"x{level + 1}", lambda k, z: values[z])
            return send(f"x{level + 1}")
        return values

    def enter(level, copies):
        unpack(f"c{level}", sent[level], arrays[level], fills)
        factor(level)
        unpack(f"x{level}", copies, [ref[f"rhs{level}"]], (0.0,))

    copies = down(0)
    own_coefficients(2)
    own_coefficients(3)
    bottom = coarsen(3)
    tiles = [pack_tile([bottom[z][k] for z in range(NZ)]) for k in range(4)]
    tiles = [tiles[3], tiles[0], tiles[1], tiles[2]]
    stage = gather_columns("gc", tiles, total_of(storage_sum), N_HALO)
    enter(1, copies)
    copies = down(1)
    stage_c = gather_rows("gc", stage, N_HALO + GY - 1)
    enter(2, copies)
    copies = down(2)
    enter(3, copies)
    values = down(3)
    tile = pack_tile(values)
    stage = gather_columns("gr", [tile], total_of(tile), N_HALO + GY - 1 + GX - 1)
    stage_r = gather_rows("gr", stage, N_HALO + 2 * (GY - 1) + GX - 1)

    for copy in stage_c:
        copy.wait_recv()
    lane = iota((16, 128), 1)
    row = iota((16, 128), 0)
    gap = (lane & 63) >= 48
    before = None
    for z in range(NZ):
        pivot = jnp.where(gap, 1.0, coarse_layer(ref["gc_r2"], 0, z))
        if z > 0:
            pivot = pivot - before * below
        inverse = 1.0 / pivot
        below = coarse_layer(ref["gc_r2"], 3, z)
        before = below * inverse
        at = slice(16 * z, 16 * z + 16)
        ref["inv4"][at, :] = inverse
        ref["g4"][at, :] = before
        ref["E4"][at, :] = coarse_layer(ref["gc_r2"], 1, z)
        ref["N4"][at, :] = coarse_layer(ref["gc_r2"], 2, z)
    storage_total = coarse_sum(ref["gc_r2"])
    for copy in stage_r:
        copy.wait_recv()
    shift = coarse_sum(ref["gr_r2"]) / storage_total
    for z in range(NZ):
        at = slice(16 * z, 16 * z + 16)
        ref["rhs4"][at, :] = coarse_layer(ref["gr_r2"], 0, z)
        ref["u4"][at, :] = jnp.broadcast_to(shift, (16, 128))

    def coarse_sweep(step, carry):
        value = None
        for z in range(NZ):
            u, east, north = coarse_at("u4", z), coarse_at("E4", z), coarse_at("N4", z)
            from_e = rot(u, -1, 0)
            from_e = jnp.where(row == 15, rot(from_e, 64, 1), from_e)
            from_w = rot(east * u, 1, 0)
            from_w = jnp.where(row == 0, rot(from_w, 64, 1), from_w)
            right = coarse_at("rhs4", z) + east * from_e + from_w + north * rot(u, -1, 1) + rot(north * u, 1, 1)
            value = right if z == 0 else right + coarse_at("g4", z - 1) * value
            ref["f4"][16 * z : 16 * z + 16, :] = value
        for z in range(NZ - 1, -1, -1):
            solved = coarse_at("f4", z) * coarse_at("inv4", z)
            value = solved if z == NZ - 1 else solved + coarse_at("g4", z) * value
            old = coarse_at("u4", z)
            ref["u4"][16 * z : 16 * z + 16, :] = old + OMEGA * (value - old)
        return carry

    lax.fori_loop(0, COARSE_SWEEPS, coarse_sweep, 0)

    columns = jnp.concatenate(
        [ref["u4"][pl.ds(0, 8, stride=16), :], ref["u4"][pl.ds(128, 8, stride=16), :]], axis=0
    )
    hit = between(iota((128, 128), 1) - 2 * (iota((128, 128), 0) - 16), 0, 2) & (iota((128, 128), 1) < 32)
    fine = exact_dot(columns, jnp.where(hit, 1.0, 0.0).astype(F32))
    for z in range(NZ):
        ref["u3"][z] = ref["u3"][z] + jnp.broadcast_to(fine[z : z + 1], (8, 128))
    for level in (3, 2, 1, 0):
        if level < 3:
            prolong(level)
        u = ref[f"u{level}"]
        pack(f"u{level}", lambda k, z: u[z, 0 : OWN_R[level], 0 : OWN_W[level]])
        unpack(f"u{level}", send(f"u{level}"), [u], (0.0,))
        sweep(level)
        sweep(level)
    for z in range(NZ):
        out[z] = ref["u0"][z, 0:16, 0:256]
    for copy in started:
        copy.wait_send()


def shards(
    newton_residual, pressure_head, conductivity, land_use, storage_table, return_table,
    well_cells, well_rates, return_cells,
):
    vmem = pl.BlockSpec(memory_space=pltpu.VMEM)
    smem = pl.BlockSpec(memory_space=pltpu.SMEM)
    wells = well_cells.shape[-1]
    return pl.pallas_call(
        kernel,
        out_shape=jax.ShapeDtypeStruct(newton_residual.shape, F32),
        in_specs=[vmem] * 4 + [smem] * 2 + [vmem] * 3,
        out_specs=vmem,
        scratch_shapes=list(PLAN.values()),
        compiler_params=pltpu.CompilerParams(
            collective_id=0, has_side_effects=True, vmem_limit_bytes=48 * 1024 * 1024
        ),
    )(
        newton_residual, pressure_head, conductivity, land_use, storage_table, return_table,
        well_cells.reshape(1, wells), well_rates.reshape(1, wells), return_cells.reshape(1, wells),
    )


def solution(mesh):
    return jax.shard_map(
        shards,
        mesh=mesh,
        in_specs=(
            P(None, "gx", "gy"),
            P(None, "gx", "gy"),
            P(None, "gx", "gy"),
            P("gx", "gy"),
            P(),
            P(),
            P("gx", "gy", None),
            P("gx", "gy", None),
            P("gx", "gy", None),
        ),
        out_specs=P(None, "gx", "gy"),
        check_vma=False,
    )
```

profile of v0, /device:TPU:1, one launch (start us, length us, event | category | flops | bytes accessed | tf_op | source)
XLA Modules:
  0.0 88.4 jit_solution(14948886691157864798)
XLA Ops:
  0.0 0.0 copy-start.7
  0.0 0.0 copy-start.8
  0.0 0.0 copy-start.4
  0.0 0.0 copy-start.5
  0.0 0.0 copy-start.6
  0.0 0.6 copy-done.7
  0.7 0.0 copy-done.8
  0.7 0.0 copy-done.4
  0.7 0.0 copy-done.5
  0.7 0.0 copy-done.6
  0.7 0.0 copy-start
  0.7 0.9 %copy-done = f32[16,16,256]{2,1,0:T(8,128)S(1)} copy-done((f32[16,16,256]{2,1,0:T(8,128)S(1)}, f32[16,16,256]{2,1,0:T(8,128)}, u32[]{:S(2)}) %copy-start) | copy-done | bytes 262168
  1.7 0.0 copy-start.1
  1.7 0.9 %copy-done.1 = f32[16,16,256]{2,1,0:T(8,128)S(1)} copy-done((f32[16,16,256]{2,1,0:T(8,128)S(1)}, f32[16,16,256]{2,1,0:T(8,128)}, u32[]{:S(2)}) %copy-start.1) | copy-done | bytes 262168
  2.6 0.0 copy-start.2
  2.6 0.9 %copy-done.2 = f32[16,16,256]{2,1,0:T(8,128)S(1)} copy-done((f32[16,16,256]{2,1,0:T(8,128)S(1)}, f32[16,16,256]{2,1,0:T(8,128)}, u32[]{:S(2)}) %copy-start.2) | copy-done | bytes 262168
  3.6 0.0 copy-start.3
  3.6 0.7 copy-done.3
  4.3 83.4 %shard_map.91 = f32[16,16,256]{2,1,0:T(8,128)S(1)} custom-call(f32[16,16,256]{2,1,0:T(8,128)S(1)} %copy-done, f32[16,16,256]{2,1,0:T(8,128)S(1)} %copy-done.1, f32[16,16,256]{2,1,0:T(8,128)S(1)} %copy-done.2, s32[16,256]{1,0:T(8,128)S(1)} %copy-done.3, f32[8]{0:T(128)S(1)} %copy-done.4, f32[8]{0:T(128)S(1)} %copy-done.5, s32[1,32]{1,0:T(1,128)S(1)} %bitcast.3, ...), custom_call_target="tpu_custom_call" | custom-call | tf_op jit(solution)/shard_map/pallas_call | solution.py:647
  87.7 0.7 copy.11
Async XLA Ops:
  0.0 0.7 copy-start.7
  0.0 0.7 copy-start.8
  0.0 0.7 copy-start.4
  0.0 0.7 copy-start.5
  0.0 0.7 copy-start.6
  0.7 0.9 %copy-start = (f32[16,16,256]{2,1,0:T(8,128)S(1)}, f32[16,16,256]{2,1,0:T(8,128)}, u32[]{:S(2)}) copy-start(f32[16,16,256]{2,1,0:T(8,128)} %residual.1) | copy-start | bytes 786436
  1.7 0.9 %copy-start.1 = (f32[16,16,256]{2,1,0:T(8,128)S(1)}, f32[16,16,256]{2,1,0:T(8,128)}, u32[]{:S(2)}) copy-start(f32[16,16,256]{2,1,0:T(8,128)} %pressure.1) | copy-start | bytes 786436
  2.6 0.9 %copy-start.2 = (f32[16,16,256]{2,1,0:T(8,128)S(1)}, f32[16,16,256]{2,1,0:T(8,128)}, u32[]{:S(2)}) copy-start(f32[16,16,256]{2,1,0:T(8,128)} %conductivity.1) | copy-start | bytes 786436
  3.6 0.7 copy-start.3
where the time goes:
time: 88.6 us; the launch traced here: 88.4 us
  Pallas kernels  83.4 us (94%)
  local copies, waits for them, and re-layouts  4.97 us (6%)
    pallas_call x1, Pallas kernels, shards(): pl.pallas_call(kernel, out_shape=jax.ShapeDtypeStruct(newton_residual.sha...  83.4 us
    unnamed x19, local copies, waits for them, and re-layouts  4.97 us

commit v1 on v0

v1 whole, which is shorter than its diff:
```python
import functools

import jax
import jax.numpy as jnp
from jax import lax
from jax.experimental import pallas as pl
from jax.experimental.pallas import tpu as pltpu
from jax.sharding import PartitionSpec as P

NZ = 16
CLASSES = 8
COARSE_SWEEPS = 12
OMEGA = 0.8
VERTICAL = 4.0
ALPHA = 0.5
F32 = jnp.float32
MESH = pl.DeviceIdType.MESH

NX = (16, 8, 4, 2)
NY = (256, 128, 64, 32)
XR = (32, 16, 32, 16)
YR = (384, 256, 128, 128)
REACH = 3
SIDES = [d for d in range(-REACH, REACH + 1) if d != 0]
GY, GX = 8, 32
N_E0 = 12
N_WIDE = 6 * REACH + 2
N_V1 = 8
B_E0 = 0
B_C2 = B_E0 + N_E0
B_X2 = B_C2 + N_WIDE
B_V1 = B_X2 + N_WIDE
N_HALO = B_V1 + N_V1
N_SEM = N_HALO + 2 * (GY - 1) + 2 * (GX - 1)
LEVEL_ARRAYS = ("E", "N", "D", "diag", "g", "inv", "rhs", "u", "f")


def rot(value, shift, axis):
    shift %= value.shape[axis]
    return value if shift == 0 else pltpu.roll(value, shift, axis)


def iota(shape, axis):
    return lax.broadcasted_iota(jnp.int32, shape, axis)


def between(index, start, count):
    return (index >= start) & (index < start + count)


def exact_dot(left, right):
    return jnp.dot(left, right, precision=lax.Precision.HIGHEST, preferred_element_type=F32)


def scratch_plan():
    plan = {}
    for level in range(4):
        for name in LEVEL_ARRAYS:
            plan[f"{name}{level}"] = pltpu.VMEM((NZ, XR[level], YR[level]), F32)
    plan["P0"] = pltpu.VMEM((NZ, XR[0], YR[0]), F32)
    plan["S0"] = pltpu.VMEM((NZ, XR[0], YR[0]), F32)
    for name in ("E4", "N4", "g4", "inv4", "rhs4", "u4", "f4"):
        plan[name] = pltpu.VMEM((NZ * 16, 128), F32)
    for name in ("ta", "tb", "tc", "td"):
        plan[name] = pltpu.VMEM((NZ, 3, 32, 128), F32)
    plan["e0_sy"] = pltpu.VMEM((2, 3, 16, 128), F32)
    plan["e0_ry"] = pltpu.VMEM((2, 3, 16, 128), F32)
    plan["e0_rc"] = pltpu.VMEM((4, 3, 8, 128), F32)
    for name, count in (("c2", 4), ("x2", 1)):
        plan[f"{name}_sx"] = pltpu.VMEM((count, 4, 8, 128), F32)
        plan[f"{name}_rx"] = pltpu.VMEM((2 * REACH + 1, count, 4, 8, 128), F32)
        plan[f"{name}_sy"] = pltpu.VMEM((2, count, 8, 128), F32)
        plan[f"{name}_ry"] = pltpu.VMEM((2, 2 * REACH + 1, count, 8, 128), F32)
    for kind in ("s", "r"):
        plan[f"v1_{kind}x"] = pltpu.VMEM((2, 8, 8, 128), F32)
        plan[f"v1_{kind}y"] = pltpu.VMEM((2, 8, 128), F32)
    plan["v1_rc"] = pltpu.VMEM((4, 8, 128), F32)
    for name in ("residual", "pressure", "conductivity"):
        plan[name] = pltpu.VMEM((NZ, NX[0], NY[0]), F32)
    plan["land_use"] = pltpu.VMEM((NX[0], NY[0]), jnp.int32)
    plan["load"] = pltpu.SemaphoreType.DMA((4,))
    for name, count in (("gc", 4), ("gr", 1)):
        plan[f"{name}_s1"] = pltpu.VMEM((count, 8, 128), F32)
        plan[f"{name}_r1"] = pltpu.VMEM((GY, count, 8, 128), F32)
        plan[f"{name}_s2"] = pltpu.VMEM((count, 8, 128), F32)
        plan[f"{name}_r2"] = pltpu.VMEM((count, GX * 8, 128), F32)
    plan["send"] = pltpu.SemaphoreType.DMA((N_SEM,))
    plan["recv"] = pltpu.SemaphoreType.DMA((N_SEM,))
    return plan


PLAN = scratch_plan()


def kernel(
    residual_in, pressure_in, conductivity_in, land_use_in, storage_table, return_table,
    well_cells, well_rates, return_cells, out, *scratch,
):
    ref = dict(zip(PLAN, scratch))
    gx = lax.axis_index("gx")
    gy = lax.axis_index("gy")

    def device(dx, dy):
        return (lax.rem(gx + (dx + GX), GX), lax.rem(gy + (dy + GY), GY))

    peers = [(dx, dy) for dx in SIDES for dy in (-1, 1)]
    peers += [(0, d) for d in range(1, GY)] + [(d, 0) for d in range(1, GX)]
    barrier = pltpu.get_barrier_semaphore()
    for dx, dy in peers:
        pl.semaphore_signal(barrier, inc=1, device_id=device(dx, dy), device_id_type=MESH)

    loads = []
    for i, (name, source) in enumerate(
        (("land_use", land_use_in), ("pressure", pressure_in), ("conductivity", conductivity_in), ("residual", residual_in))
    ):
        loads.append(pltpu.make_async_copy(source, ref[name], ref["load"].at[i]))
        loads[-1].start()
    residual, pressure, conductivity, land_use = (
        ref[name] for name in ("residual", "pressure", "conductivity", "land_use")
    )
    started = []

    def remote(src, dst, index, dx, dy):
        copy = pltpu.make_async_remote_copy(
            src_ref=src, dst_ref=dst, send_sem=ref["send"].at[index], recv_sem=ref["recv"].at[index],
            device_id=device(dx, dy), device_id_type=MESH,
        )
        copy.start()
        started.append(copy)
        return copy

    row8 = iota((8, 128), 0)
    lane8 = iota((8, 128), 1)

    def send_fine(arrays):
        sy, ry, rc = ref["e0_sy"], ref["e0_ry"], ref["e0_rc"]
        copies = []
        for k, array in enumerate(arrays):
            for side, (own, there, dx) in enumerate(((0, 16, -1), (8, 24, 1))):
                copies.append(
                    remote(
                        array.at[:, pl.ds(own, 8), pl.ds(0, 256)],
                        array.at[:, pl.ds(there, 8), pl.ds(0, 256)],
                        B_E0 + 2 * k + side, dx, 0,
                    )
                )
        lane = iota((16, 128), 1)
        for k, array in enumerate(arrays):
            low = jnp.zeros((16, 128), F32)
            high = jnp.zeros((16, 128), F32)
            for z in range(NZ):
                here = between(lane, 8 * z, 8)
                low = jnp.where(here, rot(array[z, 0:16, 0:128], 8 * z, 1), low)
                high = jnp.where(here, rot(array[z, 0:16, 128:256], 8 * z + 8, 1), high)
            sy[0, k] = low
            sy[1, k] = high
        first, last = pl.ds(0, 8), pl.ds(8, 8)
        moves = (
            (sy.at[0], ry.at[0], 0, -1),
            (sy.at[1], ry.at[1], 0, 1),
            (sy.at[0, :, first], rc.at[0], -1, -1),
            (sy.at[0, :, last], rc.at[1], 1, -1),
            (sy.at[1, :, first], rc.at[2], -1, 1),
            (sy.at[1, :, last], rc.at[3], 1, 1),
        )
        for i, (src, dst, dx, dy) in enumerate(moves):
            copies.append(remote(src, dst, B_E0 + 6 + i, dx, dy))
        return copies

    def receive_fine(copies, arrays, fills):
        for copy in copies:
            copy.wait_recv()
        ry, rc = ref["e0_ry"], ref["e0_rc"]
        lane = iota((32, 128), 1)
        for k, (array, fill) in enumerate(zip(arrays, fills)):
            north = jnp.concatenate([ry[0, k], rc[0, k], rc[1, k]], axis=0)
            south = jnp.concatenate([ry[1, k], rc[2, k], rc[3, k]], axis=0)
            for z in range(NZ):
                value = jnp.where(lane >= 120, rot(south, -8 * (z + 1), 1), fill)
                array[z, :, 256:384] = jnp.where(lane < 8, rot(north, -8 * z, 1), value)

    def send_wide(name, base, get):
        sx, sy, rx, ry = (ref[f"{name}_{kind}"] for kind in ("sx", "sy", "rx", "ry"))
        for a in range(sx.shape[0]):
            values = [get(a, z) for z in range(NZ)]
            for t in range(4):
                left = jnp.where(row8 < 4, values[t], rot(values[t + 4], 4, 0))
                right = jnp.where(row8 < 4, values[t + 8], rot(values[t + 12], 4, 0))
                tile = jnp.where(lane8 < 64, left, rot(right, 64, 1))
                sx[a, t] = tile
                rx[REACH, a, t] = tile
            low = jnp.zeros((8, 128), F32)
            high = jnp.zeros((8, 128), F32)
            for q in range(8):
                both = jnp.where(row8 < 4, values[q], rot(values[q + 8], 4, 0))
                here = between(lane8, 16 * q, 16)
                low = jnp.where(here, rot(both, 16 * q, 1), low)
                high = jnp.where(here, rot(both, 16 * q - 48, 1), high)
            sy[0, a] = low
            sy[1, a] = high
        copies = []
        for d in SIDES:
            copies.append(remote(sx, rx.at[REACH - d], base + len(copies), d, 0))
        for side, dy in ((0, -1), (1, 1)):
            for d in range(-REACH, REACH + 1):
                copies.append(remote(sy.at[side], ry.at[side, REACH - d], base + len(copies), d, dy))
        return copies

    def receive_wide(name, copies, targets, fills):
        for copy in copies:
            copy.wait_recv()
        rx, ry = ref[f"{name}_rx"], ref[f"{name}_ry"]
        empty = jnp.zeros((8, 128), F32)

        def join(first, second):
            return (
                jnp.where(row8 < 4, first, rot(second, 4, 0)),
                jnp.where(row8 < 4, rot(first, 4, 0), second),
            )

        for a, (target, fill) in enumerate(zip(targets, fills)):
            for p, (k0, k1) in enumerate(((0, 1), (2, 3), (None, -3), (-2, -1))):
                layers = [None] * NZ
                for t in range(4):
                    first = empty if k0 is None else rx[REACH + k0, a, t]
                    for i, both in enumerate(join(first, rx[REACH + k1, a, t])):
                        layers[t + 4 * i] = both
                        layers[t + 4 * i + 8] = rot(both, 64, 1)
                sides = []
                for side in (0, 1):
                    first = empty if k0 is None else ry[side, REACH + k0, a]
                    sides.append(join(first, ry[side, REACH + k1, a]))
                for z in range(NZ):
                    q = z % 8
                    north = rot(sides[0][z // 8], 64 - 16 * q, 1)
                    south = rot(sides[1][z // 8], 112 - 16 * q, 1)
                    value = jnp.where(lane8 < 80, north, jnp.where(lane8 >= 112, south, fill))
                    value = jnp.where(lane8 < 64, layers[z], value)
                    if k0 is None:
                        value = jnp.where(row8 < 4, fill, value)
                    target[z, 8 * p : 8 * p + 8, :] = value

    def send_u1():
        sx, sy, rx, ry, rc = (ref[f"v1_{kind}"] for kind in ("sx", "sy", "rx", "ry", "rc"))
        low = jnp.zeros((8, 128), F32)
        high = jnp.zeros((8, 128), F32)
        for z in range(NZ):
            u = ref["u1"][z, 0:8, 0:128]
            if z % 2 == 0:
                before = u
            else:
                sx[0, z // 2] = jnp.where(row8 < 4, before, rot(u, 4, 0))
                sx[1, z // 2] = jnp.where(row8 < 4, rot(before, 4, 0), u)
            here = between(lane8, 4 * z, 4)
            low = jnp.where(here, rot(u, 4 * z, 1), low)
            high = jnp.where(here, rot(u, 4 * z + 4, 1), high)
        sy[0] = low
        sy[1] = high
        moves = (
            (sx.at[0], rx.at[0], -1, 0),
            (sx.at[1], rx.at[1], 1, 0),
            (sy.at[0], ry.at[0], 0, -1),
            (sy.at[1], ry.at[1], 0, 1),
            (sy.at[0], rc.at[0], -1, -1),
            (sy.at[0], rc.at[1], 1, -1),
            (sy.at[1], rc.at[2], -1, 1),
            (sy.at[1], rc.at[3], 1, 1),
        )
        return [remote(src, dst, B_V1 + i, dx, dy) for i, (src, dst, dx, dy) in enumerate(moves)]

    def receive_u1(copies):
        for copy in copies:
            copy.wait_recv()
        rx, ry, rc = (ref[f"v1_{kind}"] for kind in ("rx", "ry", "rc"))
        lane = iota((16, 128), 1)
        north = jnp.concatenate([ry[0], jnp.where(row8 < 4, rc[0], rc[1])], axis=0)
        south = jnp.concatenate([ry[1], jnp.where(row8 < 4, rc[2], rc[3])], axis=0)
        u = ref["u1"]
        for z in range(NZ):
            east, west = rx[0, z // 2], rx[1, z // 2]
            if z % 2 == 0:
                value = jnp.where(row8 < 4, east, rot(west, 4, 0))
            else:
                value = jnp.where(row8 < 4, rot(east, 4, 0), west)
            u[z, 8:16, 0:128] = value
            value = jnp.where(lane >= 124, rot(south, -4 * (z + 1), 1), 0.0)
            u[z, :, 128:256] = jnp.where(lane < 4, rot(north, -4 * z, 1), value)

    def factor(level):
        diag, down, g, inv = (ref[f"{name}{level}"] for name in ("diag", "D", "g", "inv"))
        before = None
        for z in range(NZ):
            pivot = diag[z]
            if z > 0:
                pivot = pivot - before * down[z - 1]
            inverse = 1.0 / pivot
            inv[z] = inverse
            if z < NZ - 1:
                before = down[z] * inverse
                g[z] = before

    def back_substitute(level, update):
        g, inv, f = (ref[f"{name}{level}"] for name in ("g", "inv", "f"))
        value = f[NZ - 1] * inv[NZ - 1]
        update(NZ - 1, value)
        for z in range(NZ - 2, -1, -1):
            value = f[z] * inv[z] + g[z] * value
            update(z, value)

    def first_sweep(level):
        g, f, rhs, u = (ref[f"{name}{level}"] for name in ("g", "f", "rhs", "u"))
        value = rhs[0]
        f[0] = value
        for z in range(1, NZ):
            value = rhs[z] + g[z - 1] * value
            f[z] = value

        def update(z, solved):
            u[z] = OMEGA * solved

        back_substitute(level, update)

    def lateral(level, z, u):
        east, north = ref[f"E{level}"][z], ref[f"N{level}"][z]
        return (
            east * rot(u, -1, 0) + rot(east * u, 1, 0) + north * rot(u, -1, 1) + rot(north * u, 1, 1)
        )

    def sweep(level):
        g, f, rhs, u = (ref[f"{name}{level}"] for name in ("g", "f", "rhs", "u"))
        value = None
        for z in range(NZ):
            right = rhs[z] + lateral(level, z, u[z])
            value = right if z == 0 else right + g[z - 1] * value
            f[z] = value

        def update(z, solved):
            old = u[z]
            u[z] = old + OMEGA * (solved - old)

        back_substitute(level, update)

    def remainder(level, z):
        diag, down, rhs, u = (ref[f"{name}{level}"] for name in ("diag", "D", "rhs", "u"))
        here = u[z]
        value = rhs[z] + lateral(level, z, here) - diag[z] * here
        if z < NZ - 1:
            value = value + down[z] * u[z + 1]
        if z > 0:
            value = value + down[z - 1] * u[z - 1]
        return value

    PIECES = (
        ((0, 256, 256, 256), (256, 128, 64, 128)),
        ((0, 128, 128, 128),),
        ((0, 128, 96, 128),),
        ((0, 128, 128, 32),),
    )
    ROWS = (32, 8, 32, 8)

    def lane_matrix(piece, kind, transpose=False):
        _, count, turn, limit = piece
        shape = (128, count) if transpose else (count, 128)
        fine = iota(shape, 1 if transpose else 0)
        coarse = iota(shape, 0 if transpose else 1)
        hit = (((fine >> 1) + jnp.where(fine >= turn, 64, 0)) == coarse) & (fine < limit)
        if kind != "sum":
            hit = hit & ((fine & 1) == (1 if kind == "odd" else 0))
        return jnp.where(hit, 1.0, 0.0).astype(F32)

    def put_rows(buffer, level, z, value):
        for t in range(YR[level] // 128 if len(PIECES[level]) > 1 else 1):
            buffer[z, t, 0 : ROWS[level], :] = value[0 : ROWS[level], 128 * t : 128 * (t + 1)]

    def row_half(buffer, level, piece, z, odd):
        start, count = piece[0], piece[1]
        parts = []
        for t in range(start // 128, (start + count) // 128):
            rows = [buffer[z, t, pl.ds(i + odd, 8, stride=2), :] for i in range(0, ROWS[level], 16)]
            parts.append(rows[0] if len(rows) == 1 else jnp.concatenate(rows, axis=0))
        return parts[0] if len(parts) == 1 else jnp.concatenate(parts, axis=1)

    def coarse_rows(level):
        return max(8, ROWS[level] // 2)

    def layers_of(value, rows):
        return [value[rows * z : rows * (z + 1)] for z in range(NZ)]

    def keep_own(level, value, fill):
        rows, lanes = (4, 64) if level == 2 else (1, 16)
        return jnp.where((row8 < rows) & (lane8 < lanes), value, fill)

    def restrict(level):
        for z in range(NZ):
            put_rows(ref["ta"], level, z, remainder(level, z))
        pieces = []
        for piece in PIECES[level]:
            summed = jnp.concatenate(
                [
                    row_half(ref["ta"], level, piece, z, 0) + row_half(ref["ta"], level, piece, z, 1)
                    for z in range(NZ)
                ],
                axis=0,
            )
            pieces.append(layers_of(exact_dot(summed, lane_matrix(piece, "sum")), coarse_rows(level)))
        return pieces

    def coarsen(level):
        names = ("E", "N", "D", "diag")
        buffers = [ref[name] for name in ("ta", "tb", "tc", "td")]
        for z in range(NZ):
            for name, buffer in zip(names, buffers):
                put_rows(buffer, level, z, ref[f"{name}{level}"][z])
        pieces = []
        for piece in PIECES[level]:
            odd_e, sum_n, sum_d, sum_g = [], [], [], []
            for z in range(NZ):
                (e0, e1), (n0, n1), (d0, d1), (g0, g1) = (
                    [row_half(buffer, level, piece, z, odd) for odd in (0, 1)] for buffer in buffers
                )
                odd_e.append(e1)
                sum_n.append(n0 + n1)
                sum_d.append(d0 + d1)
                sum_g.append(g0 + g1 - 2.0 * e0)
            total = lane_matrix(piece, "sum")
            rows = coarse_rows(level)
            east = exact_dot(jnp.concatenate(odd_e, axis=0), total)
            down = exact_dot(jnp.concatenate(sum_d, axis=0), total)
            north = jnp.concatenate(sum_n, axis=0)
            diagonal = exact_dot(jnp.concatenate(sum_g, axis=0), total) - 2.0 * exact_dot(
                north, lane_matrix(piece, "even")
            )
            north = exact_dot(north, lane_matrix(piece, "odd"))
            pieces.append([layers_of(value, rows) for value in (east, north, down, diagonal)])
        return pieces

    def prolong(level, coarse):
        buffer = ref["ta"]
        u = ref[f"u{level}"]
        pieces = {
            0: ((0, 256, 256, 256), (256, 128, 64, 128)),
            1: ((0, 128, 128, 128), (128, 128, 128, 128)),
            2: ((0, 128, 96, 128),),
            3: ((0, 128, 96, 128),),
        }[level]
        for i, piece in enumerate(pieces):
            value = jnp.concatenate([coarse(i, z) for z in range(NZ)], axis=0)
            rows = value.shape[0] // NZ
            fine = exact_dot(value, lane_matrix(piece, "sum", transpose=True))
            start, count = piece[0], piece[1]
            for z in range(NZ):
                for t in range(count // 128):
                    for r in range(0, rows, 8):
                        part = fine[rows * z + r : rows * z + r + 8, 128 * t : 128 * (t + 1)]
                        for odd in (0, 1):
                            buffer[z, start // 128 + t, pl.ds(2 * r + odd, 8, stride=2), :] = part
        for z in range(NZ):
            add = [buffer[z, t, 0 : XR[level], :] for t in range(YR[level] // 128)]
            u[z] = u[z] + (add[0] if len(add) == 1 else jnp.concatenate(add, axis=1))

    at_sum = (lane8 == 48) & (row8 == 0)

    def pack_tile(values):
        row16 = iota((16, 128), 0)
        lane16 = iota((16, 128), 1)
        stacked = jnp.zeros((16, 128), F32)
        for z in range(NZ):
            stacked = jnp.where(row16 == z, jnp.broadcast_to(values[z][0:1], (16, 128)), stacked)
        stacked = jnp.where(lane16 < 16, stacked, 0.0)
        return rot(stacked[0:8], 16, 1) + rot(stacked[8:16], 80, 1)

    def total_of(value):
        return jnp.sum(jnp.sum(value, axis=1, keepdims=True), axis=0, keepdims=True)

    def gather_columns(name, tiles, part, base):
        for a, tile in enumerate(tiles):
            ref[f"{name}_s1"][a] = jnp.where(at_sum, part, tile) if a == 0 else tile
        return [
            remote(ref[f"{name}_s1"], ref[f"{name}_r1"].at[d], base + d - 1, 0, d) for d in range(1, GY)
        ]

    def gather_rows(name, copies, base):
        for copy in copies:
            copy.wait_recv()
        s1, r1, s2, r2 = (ref[f"{name}_{kind}"] for kind in ("s1", "r1", "s2", "r2"))
        for a in range(s1.shape[0]):
            tiles = [s1[a]] + [r1[d, a] for d in range(1, GY)]
            clean = [jnp.where(at_sum, 0.0, tiles[i]) if a == 0 else tiles[i] for i in (0, 1, GY - 1)]
            window = clean[0] + rot(clean[1], -16, 1) + rot(clean[2], 16, 1)
            if a == 0:
                parts = tiles[0]
                for tile in tiles[1:]:
                    parts = parts + tile
                window = jnp.where(at_sum, parts, window)
            s2[a] = window
            r2[a, 0:8, :] = window
        return [
            remote(s2, r2.at[:, pl.ds(8 * (GX - d), 8), :], base + d - 1, d, 0) for d in range(1, GX)
        ]

    def coarse_layer(buffer, a, z):
        sub, half = z % 8, z // 8
        pieces = [buffer[a, pl.ds(64 * i + sub, 8, stride=8), :] for i in range(4)]
        low = jnp.concatenate(pieces[0:2], axis=0)
        high = jnp.concatenate(pieces[2:4], axis=0)
        lane = iota((16, 128), 1)
        if half == 0:
            return jnp.where(lane < 64, low, rot(high, 64, 1))
        return jnp.where(lane < 64, rot(low, 64, 1), high)

    def coarse_sum(buffer):
        value = jnp.where(at_sum, buffer[0, 0:8, :], 0.0)
        for k in range(1, GX):
            value = value + jnp.where(at_sum, buffer[0, 8 * k : 8 * k + 8, :], 0.0)
        return total_of(value)

    def coarse_at(name, z):
        return ref[name][16 * z : 16 * z + 16, :]

    for copy in loads:
        copy.wait()
    use = land_use[...]
    table = jnp.zeros(use.shape, F32)
    fraction = jnp.zeros(use.shape, F32)
    for category in range(CLASSES):
        table = table + jnp.where(use == category, storage_table[category], 0.0)
        fraction = fraction + jnp.where(use == category, return_table[category], 0.0)
    cells, rates, returns = well_cells[...], well_rates[...], return_cells[...]
    wells = rates.shape[1]

    def hits(count, index):
        return iota((count, wells), 0) == index

    def outer(count, index_row, index_column):
        left = jnp.where(hits(count, index_row), rates, 0.0)
        right = jnp.where(hits(256, index_column), 1.0, 0.0).astype(F32)
        return lax.dot_general(
            left, right, (((1,), (1,)), ((), ())),
            precision=lax.Precision.HIGHEST, preferred_element_type=F32,
        )

    pumped = outer(256, cells >> 8, cells & 255)
    recharge = fraction * outer(16, returns >> 8, returns & 255)
    storage_sum = jnp.zeros((16, 256), F32)
    for z in range(NZ):
        relief = jnp.exp(ALPHA * jnp.minimum(pressure[z], 0.0))
        ref["P0"][z, 0:16, 0:256] = conductivity[z] * relief
        storage = table * relief
        ref["S0"][z, 0:16, 0:256] = storage
        storage_sum = storage_sum + storage
        source = residual[z] - pumped[16 * z : 16 * z + 16]
        if z == 0:
            source = source + recharge
        ref["rhs0"][z, 0:16, 0:256] = source
    first = [ref["P0"], ref["S0"], ref["rhs0"]]
    pl.semaphore_wait(barrier, len(peers))
    copies = send_fine(first)
    receive_fine(copies, first, (0.0, 1.0, 0.0))

    flags = [
        jnp.where(inside, 1.0, 0.0).astype(F32)
        for inside in (gx < GX - 1, gx > 0, gy < GY - 1, gy > 0)
    ]
    row = iota((32, 384), 0)
    lane = iota((32, 384), 1)
    inside = jnp.where(row < 16, 1.0, jnp.where(row < 24, flags[0], flags[1]))
    inside = inside * jnp.where(lane < 256, 1.0, jnp.where(lane < 320, flags[2], flags[3]))

    def harmonic(first_value, second_value):
        return 2.0 * first_value * second_value / (first_value + second_value + 1e-30)

    above = None
    for z in range(NZ):
        here = ref["P0"][0] * inside if z == 0 else beneath
        east = harmonic(here, rot(here, -1, 0))
        north = harmonic(here, rot(here, -1, 1))
        diagonal = ref["S0"][z] + east + rot(east, 1, 0) + north + rot(north, 1, 1)
        if z > 0:
            diagonal = diagonal + above
        if z < NZ - 1:
            beneath = ref["P0"][z + 1] * inside
            above = VERTICAL * harmonic(here, beneath)
            diagonal = diagonal + above
        else:
            above = jnp.zeros_like(here)
        ref["D0"][z] = above
        ref["E0"][z] = east
        ref["N0"][z] = north
        ref["diag0"][z] = diagonal
    factor(0)

    def place(level, names, pieces):
        for z in range(NZ):
            for k, name in enumerate(names):
                fill = 1.0 if name == "diag" else 0.0
                target = ref[f"{name}{level}"]
                if level == 1:
                    target[z, :, 0:128] = pieces[0][k][z]
                    lane = iota((16, 128), 1)
                    target[z, :, 128:256] = jnp.where((lane < 32) | (lane >= 96), pieces[1][k][z], fill)
                else:
                    lane = iota((16, 128), 1)
                    target[z] = jnp.where((lane < 48) | (lane >= 112), pieces[0][k][z], fill)

    names = ("E", "N", "D", "diag")
    fills = (0.0, 0.0, 0.0, 1.0)
    place(1, names, coarsen(0))
    (coarse2,) = coarsen(1)
    own2 = [[keep_own(2, coarse2[k][z], fills[k]) for z in range(NZ)] for k in range(4)]
    copies_c2 = send_wide("c2", B_C2, lambda k, z: own2[k][z])

    first_sweep(0)
    sweep(0)
    place(1, ("rhs",), [[piece] for piece in restrict(0)])
    factor(1)
    first_sweep(1)
    sweep(1)
    (values,) = restrict(1)
    copies_x2 = send_wide("x2", B_X2, lambda k, z: values[z])
    copies_v1 = send_u1()

    receive_wide("c2", copies_c2, [ref[f"{name}2"] for name in names], fills)
    place(3, names, coarsen(2))
    (bottom,) = coarsen(3)
    tiles = [pack_tile(bottom[k]) for k in (3, 0, 1, 2)]
    stage = gather_columns("gc", tiles, total_of(storage_sum), N_HALO)
    factor(2)
    factor(3)
    stage_c = gather_rows("gc", stage, N_HALO + GY - 1)
    receive_wide("x2", copies_x2, [ref["rhs2"]], (0.0,))
    first_sweep(2)
    sweep(2)
    place(3, ("rhs",), [[piece] for piece in restrict(2)])
    first_sweep(3)
    sweep(3)
    (values,) = restrict(3)
    tile = pack_tile(values)
    stage = gather_columns("gr", [tile], total_of(tile), N_HALO + GY - 1 + GX - 1)
    receive_u1(copies_v1)
    stage_r = gather_rows("gr", stage, N_HALO + 2 * (GY - 1) + GX - 1)

    for copy in stage_c:
        copy.wait_recv()
    lane = iota((16, 128), 1)
    row = iota((16, 128), 0)
    gap = (lane & 63) >= 48
    before = None
    for z in range(NZ):
        pivot = jnp.where(gap, 1.0, coarse_layer(ref["gc_r2"], 0, z))
        if z > 0:
            pivot = pivot - before * below
        inverse = 1.0 / pivot
        below = coarse_layer(ref["gc_r2"], 3, z)
        before = below * inverse
        at = slice(16 * z, 16 * z + 16)
        ref["inv4"][at, :] = inverse
        ref["g4"][at, :] = before
        ref["E4"][at, :] = coarse_layer(ref["gc_r2"], 1, z)
        ref["N4"][at, :] = coarse_layer(ref["gc_r2"], 2, z)
    storage_total = coarse_sum(ref["gc_r2"])
    for copy in stage_r:
        copy.wait_recv()
    shift = coarse_sum(ref["gr_r2"]) / storage_total
    for z in range(NZ):
        at = slice(16 * z, 16 * z + 16)
        ref["rhs4"][at, :] = coarse_layer(ref["gr_r2"], 0, z)
        ref["u4"][at, :] = jnp.broadcast_to(shift, (16, 128))

    def coarse_sweep(step, carry):
        value = None
        for z in range(NZ):
            u, east, north = coarse_at("u4", z), coarse_at("E4", z), coarse_at("N4", z)
            from_e = rot(u, -1, 0)
            from_e = jnp.where(row == 15, rot(from_e, 64, 1), from_e)
            from_w = rot(east * u, 1, 0)
            from_w = jnp.where(row == 0, rot(from_w, 64, 1), from_w)
            right = coarse_at("rhs4", z) + east * from_e + from_w + north * rot(u, -1, 1) + rot(north * u, 1, 1)
            value = right if z == 0 else right + coarse_at("g4", z - 1) * value
            ref["f4"][16 * z : 16 * z + 16, :] = value
        for z in range(NZ - 1, -1, -1):
            solved = coarse_at("f4", z) * coarse_at("inv4", z)
            value = solved if z == NZ - 1 else solved + coarse_at("g4", z) * value
            old = coarse_at("u4", z)
            ref["u4"][16 * z : 16 * z + 16, :] = old + OMEGA * (value - old)
        return carry

    lax.fori_loop(0, COARSE_SWEEPS, coarse_sweep, 0)

    def coarsest(_, z):
        value = coarse_at("u4", z)
        both = jnp.where(row8 < 4, value[0:8], rot(value[8:16], 64, 1))
        both = rot(both, -16, 1)
        return jnp.where((lane8 < 24) | (lane8 >= 112), both, 0.0)

    def from2(i, z):
        value = jnp.where(row8 < 6, ref["u2"][z, 0:8, :], ref["u2"][z, 24:32, :])
        return value if i == 0 else rot(value, 64, 1)

    prolong(3, coarsest)
    sweep(3)
    sweep(3)
    prolong(2, lambda i, z: ref["u3"][z])
    sweep(2)
    sweep(2)
    prolong(1, from2)
    sweep(1)
    sweep(1)
    prolong(0, lambda i, z: ref["u1"][z, :, 128 * i : 128 * (i + 1)])
    sweep(0)
    sweep(0)
    for z in range(NZ):
        out[z] = ref["u0"][z, 0:16, 0:256]
    for copy in started:
        copy.wait_send()


def shards(
    newton_residual, pressure_head, conductivity, land_use, storage_table, return_table,
    well_cells, well_rates, return_cells,
):
    vmem = pl.BlockSpec(memory_space=pltpu.VMEM)
    hbm = pl.BlockSpec(memory_space=pl.ANY)
    smem = pl.BlockSpec(memory_space=pltpu.SMEM)
    wells = well_cells.shape[-1]
    return pl.pallas_call(
        kernel,
        out_shape=jax.ShapeDtypeStruct(newton_residual.shape, F32),
        in_specs=[hbm] * 4 + [smem] * 2 + [vmem] * 3,
        out_specs=vmem,
        scratch_shapes=list(PLAN.values()),
        compiler_params=pltpu.CompilerParams(
            collective_id=0, has_side_effects=True, vmem_limit_bytes=60 * 1024 * 1024
        ),
    )(
        newton_residual, pressure_head, conductivity, land_use, storage_table, return_table,
        well_cells.reshape(1, wells), well_rates.reshape(1, wells), return_cells.reshape(1, wells),
    )


def solution(mesh):
    return jax.shard_map(
        shards,
        mesh=mesh,
        in_specs=(
            P(None, "gx", "gy"),
            P(None, "gx", "gy"),
            P(None, "gx", "gy"),
            P("gx", "gy"),
            P(),
            P(),
            P("gx", "gy", None),
            P("gx", "gy", None),
            P("gx", "gy", None),
        ),
        out_specs=P(None, "gx", "gy"),
        check_vma=False,
    )
```

time: 88.6 us -> 76.1 us (0.86)
  Pallas kernels: 83.4 us -> 74.3 us
  local copies, waits for them, and re-layouts: 4.97 us -> 1.67 us
    pallas_call x1, Pallas kernels: 83.4 us -> 74.3 us  [shards(): pl.pallas_call(kernel, out_shape=jax.ShapeDtypeStruct(newton_residual.sha...]
    unnamed x19 -> x1, local copies, waits for them, and re-layouts: 4.97 us -> 1.67 us
where the time goes in v1:
time: 76.1 us; the launch traced here: 75.9 us
  Pallas kernels  74.3 us (98%)
  local copies, waits for them, and re-layouts  1.67 us (2%)
    pallas_call x1, Pallas kernels, shards(): pl.pallas_call(kernel, out_shape=jax.ShapeDtypeStruct(newton_residual.sha...  74.3 us
    unnamed x1, local copies, waits for them, and re-layouts  1.67 us

profile of v1, /device:TPU:1, one launch (start us, length us, event | category | flops | bytes accessed | tf_op | source)
XLA Modules:
  0.0 75.9 jit_solution(7079929798435809759)
XLA Ops:
  0.0 74.3 %shard_map.91 = f32[16,16,256]{2,1,0:T(8,128)} custom-call(f32[16,16,256]{2,1,0:T(8,128)} %residual_in.1, f32[16,16,256]{2,1,0:T(8,128)} %pressure_in.1, f32[16,16,256]{2,1,0:T(8,128)} %conductivity_in.1, s32[16,256]{1,0:T(8,128)} %land_use_in.1, f32[8]{0:T(128)} %storage_table.1, f32[8]{0:T(128)} %return_table.1, s32[1,32]{1,0:T(1,128)} %bitcast.3, ...), custom_call_target="tpu_custom_call" | custom-call | tf_op jit(solution)/shard_map/pallas_call | solution.py:725
  74.3 1.7 %copy.11 = f32[16,16,256]{2,1,0:T(8,128)} copy(f32[16,16,256]{2,1,0:T(8,128)} %shard_map.91) | data formatting | bytes 524288

commit v2 on v1

--- a/solution.py
+++ b/solution.py
@@ -23,7 +23,7 @@
 REACH = 3
 SIDES = [d for d in range(-REACH, REACH + 1) if d != 0]
 GY, GX = 8, 32
-N_E0 = 12
+N_E0 = 24
 N_WIDE = 6 * REACH + 2
 N_V1 = 8
 B_E0 = 0
@@ -31,7 +31,13 @@
 B_X2 = B_C2 + N_WIDE
 B_V1 = B_X2 + N_WIDE
 N_HALO = B_V1 + N_V1
-N_SEM = N_HALO + 2 * (GY - 1) + 2 * (GX - 1)
+GZ, GXX = 8, 4
+B_GC1 = N_HALO
+B_GCZ = B_GC1 + GY - 1
+B_GCX = B_GCZ + GZ - 1
+B_GR1 = B_GCX + GZ * (GXX - 1)
+B_GR2 = B_GR1 + GY - 1
+N_SEM = B_GR2 + GX - 1
 LEVEL_ARRAYS = ("E", "N", "D", "diag", "g", "inv", "rhs", "u", "f")
 
 
@@ -57,6 +63,8 @@
     for level in range(4):
         for name in LEVEL_ARRAYS:
             plan[f"{name}{level}"] = pltpu.VMEM((NZ, XR[level], YR[level]), F32)
+    for name in ("E", "N", "g", "inv", "rhs", "u", "f"):
+        plan[f"{name}2c"] = pltpu.VMEM((NZ, 16, 128), F32)
     plan["P0"] = pltpu.VMEM((NZ, XR[0], YR[0]), F32)
     plan["S0"] = pltpu.VMEM((NZ, XR[0], YR[0]), F32)
     for name in ("E4", "N4", "g4", "inv4", "rhs4", "u4", "f4"):
@@ -132,52 +140,50 @@
     row8 = iota((8, 128), 0)
     lane8 = iota((8, 128), 1)
 
-    def send_fine(arrays):
+    def send_fine(array, k):
         sy, ry, rc = ref["e0_sy"], ref["e0_ry"], ref["e0_rc"]
+        base = B_E0 + 8 * k
         copies = []
-        for k, array in enumerate(arrays):
-            for side, (own, there, dx) in enumerate(((0, 16, -1), (8, 24, 1))):
-                copies.append(
-                    remote(
-                        array.at[:, pl.ds(own, 8), pl.ds(0, 256)],
-                        array.at[:, pl.ds(there, 8), pl.ds(0, 256)],
-                        B_E0 + 2 * k + side, dx, 0,
-                    )
+        for side, (own, there, dx) in enumerate(((0, 16, -1), (8, 24, 1))):
+            copies.append(
+                remote(
+                    array.at[:, pl.ds(own, 8), pl.ds(0, 256)],
+                    array.at[:, pl.ds(there, 8), pl.ds(0, 256)],
+                    base + side, dx, 0,
                 )
+            )
         lane = iota((16, 128), 1)
-        for k, array in enumerate(arrays):
-            low = jnp.zeros((16, 128), F32)
-            high = jnp.zeros((16, 128), F32)
-            for z in range(NZ):
-                here = between(lane, 8 * z, 8)
-                low = jnp.where(here, rot(array[z, 0:16, 0:128], 8 * z, 1), low)
-                high = jnp.where(here, rot(array[z, 0:16, 128:256], 8 * z + 8, 1), high)
-            sy[0, k] = low
-            sy[1, k] = high
+        low = jnp.zeros((16, 128), F32)
+        high = jnp.zeros((16, 128), F32)
+        for z in range(NZ):
+            here = between(lane, 8 * z, 8)
+            low = jnp.where(here, rot(array[z, 0:16, 0:128], 8 * z, 1), low)
+            high = jnp.where(here, rot(array[z, 0:16, 128:256], 8 * z + 8, 1), high)
+        sy[0, k] = low
+        sy[1, k] = high
         first, last = pl.ds(0, 8), pl.ds(8, 8)
         moves = (
-            (sy.at[0], ry.at[0], 0, -1),
-            (sy.at[1], ry.at[1], 0, 1),
-            (sy.at[0, :, first], rc.at[0], -1, -1),
-            (sy.at[0, :, last], rc.at[1], 1, -1),
-            (sy.at[1, :, first], rc.at[2], -1, 1),
-            (sy.at[1, :, last], rc.at[3], 1, 1),
+            (sy.at[0, k], ry.at[0, k], 0, -1),
+            (sy.at[1, k], ry.at[1, k], 0, 1),
+            (sy.at[0, k, first], rc.at[0, k], -1, -1),
+            (sy.at[0, k, last], rc.at[1, k], 1, -1),
+            (sy.at[1, k, first], rc.at[2, k], -1, 1),
+            (sy.at[1, k, last], rc.at[3, k], 1, 1),
         )
         for i, (src, dst, dx, dy) in enumerate(moves):
-            copies.append(remote(src, dst, B_E0 + 6 + i, dx, dy))
+            copies.append(remote(src, dst, base + 2 + i, dx, dy))
         return copies
 
-    def receive_fine(copies, arrays, fills):
+    def receive_fine(copies, array, k, fill):
         for copy in copies:
             copy.wait_recv()
         ry, rc = ref["e0_ry"], ref["e0_rc"]
         lane = iota((32, 128), 1)
-        for k, (array, fill) in enumerate(zip(arrays, fills)):
-            north = jnp.concatenate([ry[0, k], rc[0, k], rc[1, k]], axis=0)
-            south = jnp.concatenate([ry[1, k], rc[2, k], rc[3, k]], axis=0)
-            for z in range(NZ):
-                value = jnp.where(lane >= 120, rot(south, -8 * (z + 1), 1), fill)
-                array[z, :, 256:384] = jnp.where(lane < 8, rot(north, -8 * z, 1), value)
+        north = jnp.concatenate([ry[0, k], rc[0, k], rc[1, k]], axis=0)
+        south = jnp.concatenate([ry[1, k], rc[2, k], rc[3, k]], axis=0)
+        for z in range(NZ):
+            value = jnp.where(lane >= 120, rot(south, -8 * (z + 1), 1), fill)
+            array[z, :, 256:384] = jnp.where(lane < 8, rot(north, -8 * z, 1), value)
 
     def send_wide(name, base, get):
         sx, sy, rx, ry = (ref[f"{name}_{kind}"] for kind in ("sx", "sy", "rx", "ry"))
@@ -326,19 +332,25 @@
             east * rot(u, -1, 0) + rot(east * u, 1, 0) + north * rot(u, -1, 1) + rot(north * u, 1, 1)
         )
 
-    def sweep(level):
+    def sweep(level, last=None):
         g, f, rhs, u = (ref[f"{name}{level}"] for name in ("g", "f", "rhs", "u"))
+        inv = ref[f"inv{level}"]
+        rows, lanes = u.shape[1:] if last is None else last.shape[1:]
+        at = (slice(0, rows), slice(0, lanes))
         value = None
         for z in range(NZ):
-            right = rhs[z] + lateral(level, z, u[z])
-            value = right if z == 0 else right + g[z - 1] * value
-            f[z] = value
-
-        def update(z, solved):
-            old = u[z]
-            u[z] = old + OMEGA * (solved - old)
-
-        back_substitute(level, update)
+            right = rhs[(z, *at)] + lateral(level, z, u[z])[at]
+            value = right if z == 0 else right + g[(z - 1, *at)] * value
+            f[(z, *at)] = value
+        for z in range(NZ - 1, -1, -1):
+            solved = f[(z, *at)] * inv[(z, *at)]
+            value = solved if z == NZ - 1 else solved + g[(z, *at)] * value
+            old = u[(z, *at)]
+            value_new = old + OMEGA * (value - old)
+            if last is None:
+                u[z] = value_new
+            else:
+                last[z] = value_new
 
     def remainder(level, z):
         diag, down, rhs, u = (ref[f"{name}{level}"] for name in ("diag", "D", "rhs", "u"))
@@ -386,9 +398,8 @@
     def layers_of(value, rows):
         return [value[rows * z : rows * (z + 1)] for z in range(NZ)]
 
-    def keep_own(level, value, fill):
-        rows, lanes = (4, 64) if level == 2 else (1, 16)
-        return jnp.where((row8 < rows) & (lane8 < lanes), value, fill)
+    def keep_own(value, fill):
+        return jnp.where((row8 < 4) & (lane8 < 64), value, fill)
 
     def restrict(level):
         for z in range(NZ):
@@ -440,7 +451,7 @@
         pieces = {
             0: ((0, 256, 256, 256), (256, 128, 64, 128)),
             1: ((0, 128, 128, 128), (128, 128, 128, 128)),
-            2: ((0, 128, 96, 128),),
+            "2c": ((0, 128, 96, 128),),
             3: ((0, 128, 96, 128),),
         }[level]
         for i, piece in enumerate(pieces):
@@ -455,48 +466,108 @@
                         for odd in (0, 1):
                             buffer[z, start // 128 + t, pl.ds(2 * r + odd, 8, stride=2), :] = part
         for z in range(NZ):
-            add = [buffer[z, t, 0 : XR[level], :] for t in range(YR[level] // 128)]
+            add = [buffer[z, t, 0 : u.shape[1], :] for t in range(u.shape[2] // 128)]
             u[z] = u[z] + (add[0] if len(add) == 1 else jnp.concatenate(add, axis=1))
 
     at_sum = (lane8 == 48) & (row8 == 0)
 
-    def pack_tile(values):
+    def pack_tile(stacked):
+        stacked = jnp.where(iota((16, 128), 1) < 16, stacked, 0.0)
+        return rot(stacked[0:8], 16, 1) + rot(stacked[8:16], 80, 1)
+
+    def stack_layers(values):
         row16 = iota((16, 128), 0)
-        lane16 = iota((16, 128), 1)
         stacked = jnp.zeros((16, 128), F32)
         for z in range(NZ):
             stacked = jnp.where(row16 == z, jnp.broadcast_to(values[z][0:1], (16, 128)), stacked)
-        stacked = jnp.where(lane16 < 16, stacked, 0.0)
-        return rot(stacked[0:8], 16, 1) + rot(stacked[8:16], 80, 1)
+        return stacked
+
+    def coarsest_coefficients(coarse2):
+        east, north, down, diagonal = (
+            jnp.concatenate([keep_own(value, 0.0) for value in values], axis=0) for values in coarse2
+        )
+        layer, row_of = iota((16, 128), 0), iota((16, 128), 1)
+        rows = jnp.where((row_of >> 3) == layer, 1.0, 0.0).astype(F32)
+        last_row = jnp.where(row_of == 8 * layer + 3, 1.0, 0.0).astype(F32)
+        inner = jnp.where((iota((128, 128), 0) & 7) < 3, 2.0, 0.0) * east
+        fine, coarse = iota((128, 128), 0), iota((128, 128), 1)
+        hit = ((fine >> 2) == coarse) & (fine < 64)
+        lanes = jnp.where(hit, 1.0, 0.0).astype(F32)
+        last_lane = jnp.where(hit & ((fine & 3) == 3), 1.0, 0.0).astype(F32)
+        summed = exact_dot(
+            jnp.concatenate(
+                [exact_dot(last_row, east), exact_dot(rows, down), exact_dot(rows, diagonal - inner)], axis=0
+            ),
+            lanes,
+        )
+        north = exact_dot(rows, north)
+        north4 = exact_dot(north, last_lane)
+        diagonal4 = summed[32:48] - 2.0 * exact_dot(north, lanes - last_lane)
+        return diagonal4, summed[0:16], north4, summed[16:32]
 
     def total_of(value):
         return jnp.sum(jnp.sum(value, axis=1, keepdims=True), axis=0, keepdims=True)
 
     def gather_columns(name, tiles, part, base):
+        s1, r1 = ref[f"{name}_s1"], ref[f"{name}_r1"]
         for a, tile in enumerate(tiles):
-            ref[f"{name}_s1"][a] = jnp.where(at_sum, part, tile) if a == 0 else tile
-        return [
-            remote(ref[f"{name}_s1"], ref[f"{name}_r1"].at[d], base + d - 1, 0, d) for d in range(1, GY)
-        ]
-
-    def gather_rows(name, copies, base):
+            s1[a] = jnp.where(at_sum, part, tile) if a == 0 else tile
+        copies = []
+        for d in range(1, GY):
+            near = d in (1, GY - 1)
+            copies.append(
+                remote(s1 if near else s1.at[0], r1.at[d] if near else r1.at[d, 0], base + d - 1, 0, d)
+            )
+        return copies
+
+    def at_row(gx_of):
+        return pl.ds(pl.multiple_of(8 * gx_of, 8), 8)
+
+    def window_of(name, copies):
         for copy in copies:
             copy.wait_recv()
         s1, r1, s2, r2 = (ref[f"{name}_{kind}"] for kind in ("s1", "r1", "s2", "r2"))
         for a in range(s1.shape[0]):
-            tiles = [s1[a]] + [r1[d, a] for d in range(1, GY)]
-            clean = [jnp.where(at_sum, 0.0, tiles[i]) if a == 0 else tiles[i] for i in (0, 1, GY - 1)]
+            clean = [s1[a], r1[1, a], r1[GY - 1, a]]
+            if a == 0:
+                clean = [jnp.where(at_sum, 0.0, tile) for tile in clean]
             window = clean[0] + rot(clean[1], -16, 1) + rot(clean[2], 16, 1)
             if a == 0:
-                parts = tiles[0]
-                for tile in tiles[1:]:
-                    parts = parts + tile
+                parts = s1[0]
+                for d in range(1, GY):
+                    parts = parts + r1[d, 0]
                 window = jnp.where(at_sum, parts, window)
             s2[a] = window
-            r2[a, 0:8, :] = window
-        return [
-            remote(s2, r2.at[:, pl.ds(8 * (GX - d), 8), :], base + d - 1, d, 0) for d in range(1, GX)
-        ]
+            r2[a, at_row(gx), :] = window
+        return s2, r2
+
+    def gather_rows(name, copies, base):
+        s2, r2 = window_of(name, copies)
+        return [remote(s2, r2.at[:, at_row(gx), :], base + d - 1, d, 0) for d in range(1, GX)]
+
+    def gather_along_z(name, copies, base):
+        s2, r2 = window_of(name, copies)
+        return [remote(s2, r2.at[:, at_row(gx), :], base + d - 1, GXX * d, 0) for d in range(1, GZ)]
+
+    def gather_along_x(name, copies, base):
+        for copy in copies:
+            copy.wait_recv()
+        r2 = ref[f"{name}_r2"]
+        x = lax.rem(gx, GXX)
+        result = []
+        for d in range(1, GXX):
+            there = lax.rem(x + d, GXX) - x
+            for z in range(GZ):
+                rows = r2.at[:, at_row(GXX * z + x), :]
+                copy = pltpu.make_async_remote_copy(
+                    src_ref=rows, dst_ref=rows, send_sem=ref["send"].at[base + len(result)],
+                    recv_sem=ref["recv"].at[base + len(result)],
+                    device_id=(gx + there, gy), device_id_type=MESH,
+                )
+                copy.start()
+                started.append(copy)
+                result.append(copy)
+        return result
 
     def coarse_layer(buffer, a, z):
         sub, half = z % 8, z // 8
@@ -517,7 +588,7 @@
     def coarse_at(name, z):
         return ref[name][16 * z : 16 * z + 16, :]
 
-    for copy in loads:
+    for copy in loads[0:3]:
         copy.wait()
     use = land_use[...]
     table = jnp.zeros(use.shape, F32)
@@ -539,8 +610,6 @@
             precision=lax.Precision.HIGHEST, preferred_element_type=F32,
         )
 
-    pumped = outer(256, cells >> 8, cells & 255)
-    recharge = fraction * outer(16, returns >> 8, returns & 255)
     storage_sum = jnp.zeros((16, 256), F32)
     for z in range(NZ):
         relief = jnp.exp(ALPHA * jnp.minimum(pressure[z], 0.0))
@@ -548,14 +617,19 @@
         storage = table * relief
         ref["S0"][z, 0:16, 0:256] = storage
         storage_sum = storage_sum + storage
+    pl.semaphore_wait(barrier, len(peers))
+    copies_p = send_fine(ref["P0"], 0)
+    copies_s = send_fine(ref["S0"], 1)
+    loads[3].wait()
+    pumped = outer(256, cells >> 8, cells & 255)
+    recharge = fraction * outer(16, returns >> 8, returns & 255)
+    for z in range(NZ):
         source = residual[z] - pumped[16 * z : 16 * z + 16]
         if z == 0:
             source = source + recharge
         ref["rhs0"][z, 0:16, 0:256] = source
-    first = [ref["P0"], ref["S0"], ref["rhs0"]]
-    pl.semaphore_wait(barrier, len(peers))
-    copies = send_fine(first)
-    receive_fine(copies, first, (0.0, 1.0, 0.0))
+    copies_r = send_fine(ref["rhs0"], 2)
+    receive_fine(copies_p, ref["P0"], 0, 0.0)
 
     flags = [
         jnp.where(inside, 1.0, 0.0).astype(F32)
@@ -574,7 +648,7 @@
         here = ref["P0"][0] * inside if z == 0 else beneath
         east = harmonic(here, rot(here, -1, 0))
         north = harmonic(here, rot(here, -1, 1))
-        diagonal = ref["S0"][z] + east + rot(east, 1, 0) + north + rot(north, 1, 1)
+        diagonal = east + rot(east, 1, 0) + north + rot(north, 1, 1)
         if z > 0:
             diagonal = diagonal + above
         if z < NZ - 1:
@@ -587,6 +661,9 @@
         ref["E0"][z] = east
         ref["N0"][z] = north
         ref["diag0"][z] = diagonal
+    receive_fine(copies_s, ref["S0"], 1, 1.0)
+    for z in range(NZ):
+        ref["diag0"][z] = ref["diag0"][z] + ref["S0"][z]
     factor(0)
 
     def place(level, names, pieces):
@@ -606,9 +683,12 @@
     fills = (0.0, 0.0, 0.0, 1.0)
     place(1, names, coarsen(0))
     (coarse2,) = coarsen(1)
-    own2 = [[keep_own(2, coarse2[k][z], fills[k]) for z in range(NZ)] for k in range(4)]
+    own2 = [[keep_own(coarse2[k][z], fills[k]) for z in range(NZ)] for k in range(4)]
     copies_c2 = send_wide("c2", B_C2, lambda k, z: own2[k][z])
-
+    tiles = [pack_tile(value) for value in coarsest_coefficients(coarse2)]
+    stage = gather_columns("gc", tiles, total_of(storage_sum), B_GC1)
+
+    receive_fine(copies_r, ref["rhs0"], 2, 0.0)
     first_sweep(0)
     sweep(0)
     place(1, ("rhs",), [[piece] for piece in restrict(0)])
@@ -619,25 +699,28 @@
     copies_x2 = send_wide("x2", B_X2, lambda k, z: values[z])
     copies_v1 = send_u1()
 
+    stage = gather_along_z("gc", stage, B_GCZ)
+
     receive_wide("c2", copies_c2, [ref[f"{name}2"] for name in names], fills)
     place(3, names, coarsen(2))
-    (bottom,) = coarsen(3)
-    tiles = [pack_tile(bottom[k]) for k in (3, 0, 1, 2)]
-    stage = gather_columns("gc", tiles, total_of(storage_sum), N_HALO)
     factor(2)
     factor(3)
-    stage_c = gather_rows("gc", stage, N_HALO + GY - 1)
     receive_wide("x2", copies_x2, [ref["rhs2"]], (0.0,))
+    stage_c = gather_along_x("gc", stage, B_GCX)
     first_sweep(2)
     sweep(2)
     place(3, ("rhs",), [[piece] for piece in restrict(2)])
     first_sweep(3)
     sweep(3)
     (values,) = restrict(3)
-    tile = pack_tile(values)
-    stage = gather_columns("gr", [tile], total_of(tile), N_HALO + GY - 1 + GX - 1)
+    tile = pack_tile(stack_layers(values))
+    stage = gather_columns("gr", [tile], total_of(tile), B_GR1)
     receive_u1(copies_v1)
-    stage_r = gather_rows("gr", stage, N_HALO + 2 * (GY - 1) + GX - 1)
+    for name in ("E", "N", "g", "inv", "rhs", "u"):
+        for z in range(NZ):
+            ref[f"{name}2c"][z, 0:8, :] = ref[f"{name}2"][z, 0:8, :]
+            ref[f"{name}2c"][z, 8:16, :] = ref[f"{name}2"][z, 24:32, :]
+    stage_r = gather_rows("gr", stage, B_GR2)
 
     for copy in stage_c:
         copy.wait_recv()
@@ -686,30 +769,33 @@
 
     lax.fori_loop(0, COARSE_SWEEPS, coarse_sweep, 0)
 
+    turn = lax.rem(GX - gx, GX)
+
     def coarsest(_, z):
         value = coarse_at("u4", z)
-        both = jnp.where(row8 < 4, value[0:8], rot(value[8:16], 64, 1))
-        both = rot(both, -16, 1)
+        value = pltpu.roll(jnp.concatenate([value, rot(value, 64, 1)], axis=0), turn, 0)
+        both = rot(jnp.where(row8 < 4, value[0:8], value[24:32]), -16, 1)
         return jnp.where((lane8 < 24) | (lane8 >= 112), both, 0.0)
 
+    def from3(_, z):
+        return jnp.where(row8 < 4, ref["u3"][z, 0:8, :], ref["u3"][z, 8:16, :])
+
     def from2(i, z):
-        value = jnp.where(row8 < 6, ref["u2"][z, 0:8, :], ref["u2"][z, 24:32, :])
+        value = jnp.where(row8 < 6, ref["u2c"][z, 0:8, :], ref["u2c"][z, 8:16, :])
         return value if i == 0 else rot(value, 64, 1)
 
     prolong(3, coarsest)
     sweep(3)
     sweep(3)
-    prolong(2, lambda i, z: ref["u3"][z])
-    sweep(2)
-    sweep(2)
+    prolong("2c", from3)
+    sweep("2c")
+    sweep("2c")
     prolong(1, from2)
     sweep(1)
     sweep(1)
     prolong(0, lambda i, z: ref["u1"][z, :, 128 * i : 128 * (i + 1)])
     sweep(0)
-    sweep(0)
-    for z in range(NZ):
-        out[z] = ref["u0"][z, 0:16, 0:256]
+    sweep(0, last=out)
     for copy in started:
         copy.wait_send()
 
@@ -719,7 +805,7 @@
     well_cells, well_rates, return_cells,
 ):
     vmem = pl.BlockSpec(memory_space=pltpu.VMEM)
-    hbm = pl.BlockSpec(memory_space=pl.ANY)
+    hbm = pl.BlockSpec(memory_space=pltpu.HBM)
     smem = pl.BlockSpec(memory_space=pltpu.SMEM)
     wells = well_cells.shape[-1]
     return pl.pallas_call(
@@ -729,7 +815,7 @@
         out_specs=vmem,
         scratch_shapes=list(PLAN.values()),
         compiler_params=pltpu.CompilerParams(
-            collective_id=0, has_side_effects=True, vmem_limit_bytes=60 * 1024 * 1024
+            collective_id=0, has_side_effects=True, vmem_limit_bytes=36 * 1024 * 1024
         ),
     )(
         newton_residual, pressure_head, conductivity, land_use, storage_table, return_table,

time: 76.1 us -> 66.8 us (0.88)
  Pallas kernels: 74.3 us -> 61.5 us
  local copies, waits for them, and re-layouts: 1.67 us -> 4.97 us
    pallas_call x1, Pallas kernels: 74.3 us -> 61.5 us  [shards(): pl.pallas_call(kernel, out_shape=jax.ShapeDtypeStruct(newton_residual.sha...]
    unnamed x1 -> x19, local copies, waits for them, and re-layouts: 1.67 us -> 4.97 us
where the time goes in v2:
time: 66.8 us; the launch traced here: 66.6 us
  Pallas kernels  61.5 us (92%)
  local copies, waits for them, and re-layouts  4.97 us (7%)
    pallas_call x1, Pallas kernels, shards(): pl.pallas_call(kernel, out_shape=jax.ShapeDtypeStruct(newton_residual.sha...  61.5 us
    unnamed x19, local copies, waits for them, and re-layouts  4.97 us

profile of v2, /device:TPU:1, one launch (start us, length us, event | category | flops | bytes accessed | tf_op | source)
XLA Modules:
  0.0 66.6 jit_solution(15714796296961979057)
XLA Ops:
  0.0 0.0 copy-start.7
  0.0 0.0 copy-start.8
  0.0 0.0 copy-start.4
  0.0 0.0 copy-start.5
  0.0 0.0 copy-start.6
  0.0 0.6 copy-done.7
  0.7 0.0 copy-done.8
  0.7 0.0 copy-done.4
  0.7 0.0 copy-done.5
  0.7 0.0 copy-done.6
  0.7 0.0 copy-start
  0.7 0.9 %copy-done = f32[16,16,256]{2,1,0:T(8,128)S(1)} copy-done((f32[16,16,256]{2,1,0:T(8,128)S(1)}, f32[16,16,256]{2,1,0:T(8,128)}, u32[]{:S(2)}) %copy-start) | copy-done | bytes 262168
  1.7 0.0 copy-start.1
  1.7 0.9 %copy-done.1 = f32[16,16,256]{2,1,0:T(8,128)S(1)} copy-done((f32[16,16,256]{2,1,0:T(8,128)S(1)}, f32[16,16,256]{2,1,0:T(8,128)}, u32[]{:S(2)}) %copy-start.1) | copy-done | bytes 262168
  2.6 0.0 copy-start.2
  2.6 0.9 %copy-done.2 = f32[16,16,256]{2,1,0:T(8,128)S(1)} copy-done((f32[16,16,256]{2,1,0:T(8,128)S(1)}, f32[16,16,256]{2,1,0:T(8,128)}, u32[]{:S(2)}) %copy-start.2) | copy-done | bytes 262168
  3.6 0.0 copy-start.3
  3.6 0.7 %copy-done.3 = s32[16,256]{1,0:T(8,128)S(1)} copy-done((s32[16,256]{1,0:T(8,128)S(1)}, s32[16,256]{1,0:T(8,128)}, u32[]{:S(2)}) %copy-start.3) | copy-done | bytes 16408
  4.3 61.5 %shard_map.91 = f32[16,16,256]{2,1,0:T(8,128)S(1)} custom-call(f32[16,16,256]{2,1,0:T(8,128)S(1)} %copy-done, f32[16,16,256]{2,1,0:T(8,128)S(1)} %copy-done.1, f32[16,16,256]{2,1,0:T(8,128)S(1)} %copy-done.2, s32[16,256]{1,0:T(8,128)S(1)} %copy-done.3, f32[8]{0:T(128)S(1)} %copy-done.4, f32[8]{0:T(128)S(1)} %copy-done.5, s32[1,32]{1,0:T(1,128)S(1)} %bitcast.3, ...), custom_call_target="tpu_custom_call" | custom-call | tf_op jit(solution)/shard_map/pallas_call | solution.py:811
  65.8 0.7 %copy.11 = f32[16,16,256]{2,1,0:T(8,128)} copy(f32[16,16,256]{2,1,0:T(8,128)S(1)} %shard_map.91) | data formatting | bytes 524288
Async XLA Ops:
  0.0 0.7 copy-start.7
  0.0 0.7 %copy-start.8 = (s32[1,1,32]{2,1,0:T(1,128)S(1)}, s32[1,1,32]{2,1,0:T(1,128)}, u32[]{:S(2)}) copy-start(s32[1,1,32]{2,1,0:T(1,128)} %param.17) | copy-start | bytes 388
  0.0 0.7 %copy-start.4 = (f32[8]{0:T(128)S(1)}, f32[8]{0:T(128)}, u32[]{:S(2)}) copy-start(f32[8]{0:T(128)} %storage_table.1) | copy-start | bytes 100
  0.0 0.7 %copy-start.5 = (f32[8]{0:T(128)S(1)}, f32[8]{0:T(128)}, u32[]{:S(2)}) copy-start(f32[8]{0:T(128)} %return_table.1) | copy-start | bytes 100
  0.0 0.7 %copy-start.6 = (s32[1,1,32]{2,1,0:T(1,128)S(1)}, s32[1,1,32]{2,1,0:T(1,128)}, u32[]{:S(2)}) copy-start(s32[1,1,32]{2,1,0:T(1,128)} %param.15) | copy-start | bytes 388
  0.7 0.9 %copy-start = (f32[16,16,256]{2,1,0:T(8,128)S(1)}, f32[16,16,256]{2,1,0:T(8,128)}, u32[]{:S(2)}) copy-start(f32[16,16,256]{2,1,0:T(8,128)} %residual_in.1) | copy-start | bytes 786436
  1.7 0.9 %copy-start.1 = (f32[16,16,256]{2,1,0:T(8,128)S(1)}, f32[16,16,256]{2,1,0:T(8,128)}, u32[]{:S(2)}) copy-start(f32[16,16,256]{2,1,0:T(8,128)} %pressure_in.1) | copy-start | bytes 786436
  2.6 0.9 %copy-start.2 = (f32[16,16,256]{2,1,0:T(8,128)S(1)}, f32[16,16,256]{2,1,0:T(8,128)}, u32[]{:S(2)}) copy-start(f32[16,16,256]{2,1,0:T(8,128)} %conductivity_in.1) | copy-start | bytes 786436
  3.6 0.7 %copy-start.3 = (s32[16,256]{1,0:T(8,128)S(1)}, s32[16,256]{1,0:T(8,128)}, u32[]{:S(2)}) copy-start(s32[16,256]{1,0:T(8,128)} %land_use_in.1) | copy-start | bytes 49156

commit v3 on v2

--- a/solution.py
+++ b/solution.py
@@ -74,6 +74,9 @@
     plan["e0_sy"] = pltpu.VMEM((2, 3, 16, 128), F32)
     plan["e0_ry"] = pltpu.VMEM((2, 3, 16, 128), F32)
     plan["e0_rc"] = pltpu.VMEM((4, 3, 8, 128), F32)
+    for kind in ("s", "r"):
+        plan[f"e0_{kind}a"] = pltpu.VMEM((2, NZ, 8, 256), F32)
+        plan[f"e0_{kind}b"] = pltpu.VMEM((2, NZ // 2, 8, 256), F32)
     for name, count in (("c2", 4), ("x2", 1)):
         plan[f"{name}_sx"] = pltpu.VMEM((count, 4, 8, 128), F32)
         plan[f"{name}_rx"] = pltpu.VMEM((2 * REACH + 1, count, 4, 8, 128), F32)
@@ -86,6 +89,7 @@
     for name in ("residual", "pressure", "conductivity"):
         plan[name] = pltpu.VMEM((NZ, NX[0], NY[0]), F32)
     plan["land_use"] = pltpu.VMEM((NX[0], NY[0]), jnp.int32)
+    plan["relay"] = pltpu.SemaphoreType.REGULAR((4,))
     plan["load"] = pltpu.SemaphoreType.DMA((4,))
     for name, count in (("gc", 4), ("gr", 1)):
         plan[f"{name}_s1"] = pltpu.VMEM((count, 8, 128), F32)
@@ -111,8 +115,18 @@
     def device(dx, dy):
         return (lax.rem(gx + (dx + GX), GX), lax.rem(gy + (dy + GY), GY))
 
-    peers = [(dx, dy) for dx in SIDES for dy in (-1, 1)]
-    peers += [(0, d) for d in range(1, GY)] + [(d, 0) for d in range(1, GX)]
+    peers = [(dx, dy) for dx in (-1, 0, 1) for dy in (-1, 0, 1) if (dx, dy) != (0, 0)]
+    relays = (peers, [(2 * dx, 2 * dy) for dx, dy in peers], [(-4, 0), (4, 0)], [(-8, 0), (8, 0)])
+
+    def relay(stage):
+        for dx, dy in relays[stage]:
+            pl.semaphore_signal(
+                ref["relay"].at[stage], inc=1, device_id=device(dx, dy), device_id_type=MESH
+            )
+
+    def await_relay(stage):
+        pl.semaphore_wait(ref["relay"].at[stage], len(relays[stage]))
+
     barrier = pltpu.get_barrier_semaphore()
     for dx, dy in peers:
         pl.semaphore_signal(barrier, inc=1, device_id=device(dx, dy), device_id_type=MESH)
@@ -140,18 +154,62 @@
     row8 = iota((8, 128), 0)
     lane8 = iota((8, 128), 1)
 
-    def send_fine(array, k):
-        sy, ry, rc = ref["e0_sy"], ref["e0_ry"], ref["e0_rc"]
-        base = B_E0 + 8 * k
+    def send_permeable(array):
         copies = []
         for side, (own, there, dx) in enumerate(((0, 16, -1), (8, 24, 1))):
             copies.append(
                 remote(
                     array.at[:, pl.ds(own, 8), pl.ds(0, 256)],
                     array.at[:, pl.ds(there, 8), pl.ds(0, 256)],
-                    base + side, dx, 0,
+                    B_E0 + side, dx, 0,
                 )
             )
+        return copies
+
+    row_wide = iota((8, 256), 0)
+
+    def pack_rows(storage, source):
+        sa, sb = ref["e0_sa"], ref["e0_sb"]
+        for z in range(NZ):
+            for side in (0, 1):
+                at = slice(8 * side, 8 * side + 8)
+                kept, moved = storage[z, at, 0:256], source[z, at, 0:256]
+                if side == 0:
+                    sa[side, z] = jnp.where(row_wide < 6, kept, rot(moved, 6, 0))
+                else:
+                    sa[side, z] = jnp.where(row_wide >= 2, kept, rot(moved, 2, 0))
+                if z % 2 == 1:
+                    first = source[z - 1, at, 0:256]
+                    sb[side, z // 2] = jnp.where(row_wide < 4, rot(first, -2, 0), rot(moved, 2, 0))
+
+    def send_rows():
+        sa, sb, ra, rb = (ref[f"e0_{kind}"] for kind in ("sa", "sb", "ra", "rb"))
+        copies = []
+        for side, dx in ((0, -1), (1, 1)):
+            copies.append(remote(sa.at[side], ra.at[side], B_E0 + 20 + side, dx, 0))
+            copies.append(remote(sb.at[side], rb.at[side], B_E0 + 22 + side, dx, 0))
+        return copies
+
+    def receive_rows(copies, storage, source):
+        for copy in copies:
+            copy.wait_recv()
+        ra, rb = ref["e0_ra"], ref["e0_rb"]
+        middle = (row_wide >= 2) & (row_wide < 6)
+        for z in range(NZ):
+            shift = 2 if z % 2 == 0 else -2
+            for side in (0, 1):
+                at = slice(16 + 8 * side, 24 + 8 * side)
+                tile, rest = ra[side, z], rot(rb[side, z // 2], shift, 0)
+                if side == 0:
+                    storage[z, at, 0:256] = jnp.where(row_wide < 6, tile, 1.0)
+                    near = jnp.where(row_wide < 2, rot(tile, -6, 0), 0.0)
+                else:
+                    storage[z, at, 0:256] = jnp.where(row_wide >= 2, tile, 1.0)
+                    near = jnp.where(row_wide >= 6, rot(tile, -2, 0), 0.0)
+                source[z, at, 0:256] = jnp.where(middle, rest, near)
+
+    def pack_columns(array, k):
+        sy = ref["e0_sy"]
         lane = iota((16, 128), 1)
         low = jnp.zeros((16, 128), F32)
         high = jnp.zeros((16, 128), F32)
@@ -161,6 +219,11 @@
             high = jnp.where(here, rot(array[z, 0:16, 128:256], 8 * z + 8, 1), high)
         sy[0, k] = low
         sy[1, k] = high
+
+    def send_columns(k):
+        sy, ry, rc = ref["e0_sy"], ref["e0_ry"], ref["e0_rc"]
+        base = B_E0 + 2 + 6 * k
+        copies = []
         first, last = pl.ds(0, 8), pl.ds(8, 8)
         moves = (
             (sy.at[0, k], ry.at[0, k], 0, -1),
@@ -171,10 +234,10 @@
             (sy.at[1, k, last], rc.at[3, k], 1, 1),
         )
         for i, (src, dst, dx, dy) in enumerate(moves):
-            copies.append(remote(src, dst, base + 2 + i, dx, dy))
+            copies.append(remote(src, dst, base + i, dx, dy))
         return copies
 
-    def receive_fine(copies, array, k, fill):
+    def receive_columns(copies, array, k, fill):
         for copy in copies:
             copy.wait_recv()
         ry, rc = ref["e0_ry"], ref["e0_rc"]
@@ -185,8 +248,8 @@
             value = jnp.where(lane >= 120, rot(south, -8 * (z + 1), 1), fill)
             array[z, :, 256:384] = jnp.where(lane < 8, rot(north, -8 * z, 1), value)
 
-    def send_wide(name, base, get):
-        sx, sy, rx, ry = (ref[f"{name}_{kind}"] for kind in ("sx", "sy", "rx", "ry"))
+    def pack_wide(name, get):
+        sx, sy, rx = (ref[f"{name}_{kind}"] for kind in ("sx", "sy", "rx"))
         for a in range(sx.shape[0]):
             values = [get(a, z) for z in range(NZ)]
             for t in range(4):
@@ -204,15 +267,23 @@
                 high = jnp.where(here, rot(both, 16 * q - 48, 1), high)
             sy[0, a] = low
             sy[1, a] = high
+
+    def send_wide(name, base):
+        return send_wide_to(name, base, [d for d in SIDES if abs(d) < REACH])
+
+    def send_wide_to(name, base, sides):
+        sx, sy, rx, ry = (ref[f"{name}_{kind}"] for kind in ("sx", "sy", "rx", "ry"))
+        far = REACH in sides
         copies = []
-        for d in SIDES:
-            copies.append(remote(sx, rx.at[REACH - d], base + len(copies), d, 0))
+        for d in sides:
+            copies.append(remote(sx, rx.at[REACH - d], base + SIDES.index(d), d, 0))
         for side, dy in ((0, -1), (1, 1)):
-            for d in range(-REACH, REACH + 1):
-                copies.append(remote(sy.at[side], ry.at[side, REACH - d], base + len(copies), d, dy))
+            for d in sides if far else sides + [0]:
+                index = 2 * REACH + side * (2 * REACH + 1) + d + REACH
+                copies.append(remote(sy.at[side], ry.at[side, REACH - d], base + index, d, dy))
         return copies
 
-    def receive_wide(name, copies, targets, fills):
+    def receive_wide(name, copies, targets, fills, far):
         for copy in copies:
             copy.wait_recv()
         rx, ry = ref[f"{name}_rx"], ref[f"{name}_ry"]
@@ -225,17 +296,26 @@
             )
 
         for a, (target, fill) in enumerate(zip(targets, fills)):
-            for p, (k0, k1) in enumerate(((0, 1), (2, 3), (None, -3), (-2, -1))):
+            tiles = {0: (0, 1), 1: (2, None), 2: (None, None), 3: (-2, -1)}
+            if far:
+                tiles = {1: (2, 3), 2: (None, -3)}
+            for p, (k0, k1) in tiles.items():
+                if k0 is None and k1 is None:
+                    for z in range(NZ):
+                        target[z, 8 * p : 8 * p + 8, :] = jnp.full((8, 128), fill, F32)
+                    continue
                 layers = [None] * NZ
                 for t in range(4):
                     first = empty if k0 is None else rx[REACH + k0, a, t]
-                    for i, both in enumerate(join(first, rx[REACH + k1, a, t])):
+                    second = empty if k1 is None else rx[REACH + k1, a, t]
+                    for i, both in enumerate(join(first, second)):
                         layers[t + 4 * i] = both
                         layers[t + 4 * i + 8] = rot(both, 64, 1)
                 sides = []
                 for side in (0, 1):
                     first = empty if k0 is None else ry[side, REACH + k0, a]
-                    sides.append(join(first, ry[side, REACH + k1, a]))
+                    second = empty if k1 is None else ry[side, REACH + k1, a]
+                    sides.append(join(first, second))
                 for z in range(NZ):
                     q = z % 8
                     north = rot(sides[0][z // 8], 64 - 16 * q, 1)
@@ -244,6 +324,8 @@
                     value = jnp.where(lane8 < 64, layers[z], value)
                     if k0 is None:
                         value = jnp.where(row8 < 4, fill, value)
+                    if k1 is None:
+                        value = jnp.where(row8 < 4, value, fill)
                     target[z, 8 * p : 8 * p + 8, :] = value
 
     def send_u1():
@@ -380,20 +462,23 @@
             hit = hit & ((fine & 1) == (1 if kind == "odd" else 0))
         return jnp.where(hit, 1.0, 0.0).astype(F32)
 
-    def put_rows(buffer, level, z, value):
-        for t in range(YR[level] // 128 if len(PIECES[level]) > 1 else 1):
-            buffer[z, t, 0 : ROWS[level], :] = value[0 : ROWS[level], 128 * t : 128 * (t + 1)]
-
-    def row_half(buffer, level, piece, z, odd):
+    def put_rows(buffer, rows, z, value):
+        for t in range(value.shape[1] // 128):
+            buffer[z, t, 0:rows, :] = value[0:rows, 128 * t : 128 * (t + 1)]
+
+    def row_half(buffer, count_rows, piece, z, odd):
         start, count = piece[0], piece[1]
         parts = []
         for t in range(start // 128, (start + count) // 128):
-            rows = [buffer[z, t, pl.ds(i + odd, 8, stride=2), :] for i in range(0, ROWS[level], 16)]
+            rows = [buffer[z, t, pl.ds(i + odd, 8, stride=2), :] for i in range(0, count_rows, 16)]
             parts.append(rows[0] if len(rows) == 1 else jnp.concatenate(rows, axis=0))
         return parts[0] if len(parts) == 1 else jnp.concatenate(parts, axis=1)
 
-    def coarse_rows(level):
-        return max(8, ROWS[level] // 2)
+    def coarse_rows(rows):
+        return max(8, rows // 2)
+
+    def lanes_of(level):
+        return sum(piece[1] for piece in PIECES[level])
 
     def layers_of(value, rows):
         return [value[rows * z : rows * (z + 1)] for z in range(NZ)]
@@ -403,38 +488,43 @@
 
     def restrict(level):
         for z in range(NZ):
-            put_rows(ref["ta"], level, z, remainder(level, z))
+            put_rows(ref["ta"], ROWS[level], z, remainder(level, z)[:, 0 : lanes_of(level)])
         pieces = []
         for piece in PIECES[level]:
             summed = jnp.concatenate(
                 [
-                    row_half(ref["ta"], level, piece, z, 0) + row_half(ref["ta"], level, piece, z, 1)
+                    row_half(ref["ta"], ROWS[level], piece, z, 0) + row_half(ref["ta"], ROWS[level], piece, z, 1)
                     for z in range(NZ)
                 ],
                 axis=0,
             )
-            pieces.append(layers_of(exact_dot(summed, lane_matrix(piece, "sum")), coarse_rows(level)))
+            pieces.append(layers_of(exact_dot(summed, lane_matrix(piece, "sum")), coarse_rows(ROWS[level])))
         return pieces
 
-    def coarsen(level):
+    def coarsen(level, own=False):
+        rows_fine = 16 if own else ROWS[level]
+        lanes = 256 if own else lanes_of(level)
         names = ("E", "N", "D", "diag")
         buffers = [ref[name] for name in ("ta", "tb", "tc", "td")]
         for z in range(NZ):
             for name, buffer in zip(names, buffers):
-                put_rows(buffer, level, z, ref[f"{name}{level}"][z])
+                value = ref[f"{name}{level}"][z, 0:rows_fine, 0:lanes]
+                if own and name == "diag":
+                    value = value + ref["S0"][z, 0:rows_fine, 0:lanes]
+                put_rows(buffer, rows_fine, z, value)
         pieces = []
-        for piece in PIECES[level]:
+        for piece in PIECES[level][0:1] if own else PIECES[level]:
             odd_e, sum_n, sum_d, sum_g = [], [], [], []
             for z in range(NZ):
                 (e0, e1), (n0, n1), (d0, d1), (g0, g1) = (
-                    [row_half(buffer, level, piece, z, odd) for odd in (0, 1)] for buffer in buffers
+                    [row_half(buffer, rows_fine, piece, z, odd) for odd in (0, 1)] for buffer in buffers
                 )
                 odd_e.append(e1)
                 sum_n.append(n0 + n1)
                 sum_d.append(d0 + d1)
                 sum_g.append(g0 + g1 - 2.0 * e0)
             total = lane_matrix(piece, "sum")
-            rows = coarse_rows(level)
+            rows = coarse_rows(rows_fine)
             east = exact_dot(jnp.concatenate(odd_e, axis=0), total)
             down = exact_dot(jnp.concatenate(sum_d, axis=0), total)
             north = jnp.concatenate(sum_n, axis=0)
@@ -588,7 +678,7 @@
     def coarse_at(name, z):
         return ref[name][16 * z : 16 * z + 16, :]
 
-    for copy in loads[0:3]:
+    for copy in loads:
         copy.wait()
     use = land_use[...]
     table = jnp.zeros(use.shape, F32)
@@ -617,10 +707,6 @@
         storage = table * relief
         ref["S0"][z, 0:16, 0:256] = storage
         storage_sum = storage_sum + storage
-    pl.semaphore_wait(barrier, len(peers))
-    copies_p = send_fine(ref["P0"], 0)
-    copies_s = send_fine(ref["S0"], 1)
-    loads[3].wait()
     pumped = outer(256, cells >> 8, cells & 255)
     recharge = fraction * outer(16, returns >> 8, returns & 255)
     for z in range(NZ):
@@ -628,8 +714,18 @@
         if z == 0:
             source = source + recharge
         ref["rhs0"][z, 0:16, 0:256] = source
-    copies_r = send_fine(ref["rhs0"], 2)
-    receive_fine(copies_p, ref["P0"], 0, 0.0)
+    for k, name in enumerate(("P0", "S0", "rhs0")):
+        pack_columns(ref[name], k)
+    pack_rows(ref["S0"], ref["rhs0"])
+    pl.semaphore_wait(barrier, len(peers))
+    copies_p = send_permeable(ref["P0"]) + send_columns(0)
+    copies_rows = send_rows()
+    copies_s = send_columns(1)
+    copies_r = send_columns(2)
+    relay(0)
+    await_relay(0)
+    relay(1)
+    receive_columns(copies_p, ref["P0"], 0, 0.0)
 
     flags = [
         jnp.where(inside, 1.0, 0.0).astype(F32)
@@ -661,11 +757,6 @@
         ref["E0"][z] = east
         ref["N0"][z] = north
         ref["diag0"][z] = diagonal
-    receive_fine(copies_s, ref["S0"], 1, 1.0)
-    for z in range(NZ):
-        ref["diag0"][z] = ref["diag0"][z] + ref["S0"][z]
-    factor(0)
-
     def place(level, names, pieces):
         for z in range(NZ):
             for k, name in enumerate(names):
@@ -681,46 +772,80 @@
 
     names = ("E", "N", "D", "diag")
     fills = (0.0, 0.0, 0.0, 1.0)
-    place(1, names, coarsen(0))
+    (own1,) = coarsen(0, own=True)
+    for k, name in enumerate(names):
+        for z in range(NZ):
+            ref[f"{name}1"][z, 0:8, 0:128] = own1[k][z]
     (coarse2,) = coarsen(1)
     own2 = [[keep_own(coarse2[k][z], fills[k]) for z in range(NZ)] for k in range(4)]
-    copies_c2 = send_wide("c2", B_C2, lambda k, z: own2[k][z])
+    pack_wide("c2", lambda k, z: own2[k][z])
     tiles = [pack_tile(value) for value in coarsest_coefficients(coarse2)]
+    await_relay(1)
+    relay(2)
+    copies_c2 = send_wide("c2", B_C2)
     stage = gather_columns("gc", tiles, total_of(storage_sum), B_GC1)
 
-    receive_fine(copies_r, ref["rhs0"], 2, 0.0)
+    receive_rows(copies_rows, ref["S0"], ref["rhs0"])
+    receive_columns(copies_s, ref["S0"], 1, 1.0)
+    for z in range(NZ):
+        ref["diag0"][z] = ref["diag0"][z] + ref["S0"][z]
+    factor(0)
+    place(1, names, coarsen(0))
+    factor(1)
+
+    receive_columns(copies_r, ref["rhs0"], 2, 0.0)
     first_sweep(0)
     sweep(0)
+    first_sweep(0)
+    sweep(0)
+    await_relay(2)
+    relay(3)
     place(1, ("rhs",), [[piece] for piece in restrict(0)])
-    factor(1)
     first_sweep(1)
     sweep(1)
     (values,) = restrict(1)
-    copies_x2 = send_wide("x2", B_X2, lambda k, z: values[z])
+    pack_wide("x2", lambda k, z: values[z])
+    copies_x2 = send_wide("x2", B_X2)
     copies_v1 = send_u1()
-
+    far_sides = [-REACH, REACH]
+    copies_far = send_wide_to("c2", B_C2, far_sides)
+    copies_far_x = send_wide_to("x2", B_X2, far_sides)
+
+    await_relay(3)
     stage = gather_along_z("gc", stage, B_GCZ)
 
-    receive_wide("c2", copies_c2, [ref[f"{name}2"] for name in names], fills)
-    place(3, names, coarsen(2))
-    factor(2)
-    factor(3)
-    receive_wide("x2", copies_x2, [ref["rhs2"]], (0.0,))
+    two = [ref[f"{name}2"] for name in names]
+    receive_wide("c2", copies_c2, two, fills, False)
+
+    def prepare23():
+        place(3, names, coarsen(2))
+        factor(2)
+        factor(3)
+
+    def down23():
+        first_sweep(2)
+        sweep(2)
+        place(3, ("rhs",), [[piece] for piece in restrict(2)])
+        first_sweep(3)
+        sweep(3)
+
+    prepare23()
+    receive_wide("x2", copies_x2, [ref["rhs2"]], (0.0,), False)
     stage_c = gather_along_x("gc", stage, B_GCX)
-    first_sweep(2)
-    sweep(2)
-    place(3, ("rhs",), [[piece] for piece in restrict(2)])
-    first_sweep(3)
-    sweep(3)
+    down23()
     (values,) = restrict(3)
     tile = pack_tile(stack_layers(values))
     stage = gather_columns("gr", [tile], total_of(tile), B_GR1)
     receive_u1(copies_v1)
+    stage_r = gather_rows("gr", stage, B_GR2)
+    receive_wide("c2", copies_far, two, fills, True)
+    receive_wide("x2", copies_far_x, [ref["rhs2"]], (0.0,), True)
+    prepare23()
+    down23()
     for name in ("E", "N", "g", "inv", "rhs", "u"):
         for z in range(NZ):
             ref[f"{name}2c"][z, 0:8, :] = ref[f"{name}2"][z, 0:8, :]
             ref[f"{name}2c"][z, 8:16, :] = ref[f"{name}2"][z, 24:32, :]
-    stage_r = gather_rows("gr", stage, B_GR2)
 
     for copy in stage_c:
         copy.wait_recv()

time: 66.8 us -> 64.3 us (0.963)
  Pallas kernels: 61.5 us -> 58.4 us
    pallas_call x1, Pallas kernels: 61.5 us -> 58.4 us  [shards(): pl.pallas_call(kernel, out_shape=jax.ShapeDtypeStruct(newton_residual.sha...]
where the time goes in v3:
time: 64.3 us; the launch traced here: 63.4 us
  Pallas kernels  58.4 us (91%)
  local copies, waits for them, and re-layouts  4.97 us (8%)
    pallas_call x1, Pallas kernels, shards(): pl.pallas_call(kernel, out_shape=jax.ShapeDtypeStruct(newton_residual.sha...  58.4 us
    unnamed x19, local copies, waits for them, and re-layouts  4.97 us

profile of v3, /device:TPU:1, one launch (start us, length us, event | category | flops | bytes accessed | tf_op | source)
XLA Modules:
  0.0 63.4 jit_solution(15315675503606537359)
XLA Ops:
  0.0 0.0 copy-start.7
  0.0 0.0 copy-start.8
  0.0 0.0 copy-start.4
  0.0 0.0 copy-start.5
  0.0 0.0 copy-start.6
  0.0 0.6 copy-done.7
  0.7 0.0 copy-done.8
  0.7 0.0 copy-done.4
  0.7 0.0 copy-done.5
  0.7 0.0 copy-done.6
  0.7 0.0 copy-start
  0.7 0.9 %copy-done = f32[16,16,256]{2,1,0:T(8,128)S(1)} copy-done((f32[16,16,256]{2,1,0:T(8,128)S(1)}, f32[16,16,256]{2,1,0:T(8,128)}, u32[]{:S(2)}) %copy-start) | copy-done | bytes 262168
  1.7 0.0 copy-start.1
  1.7 0.9 %copy-done.1 = f32[16,16,256]{2,1,0:T(8,128)S(1)} copy-done((f32[16,16,256]{2,1,0:T(8,128)S(1)}, f32[16,16,256]{2,1,0:T(8,128)}, u32[]{:S(2)}) %copy-start.1) | copy-done | bytes 262168
  2.6 0.0 copy-start.2
  2.6 0.9 %copy-done.2 = f32[16,16,256]{2,1,0:T(8,128)S(1)} copy-done((f32[16,16,256]{2,1,0:T(8,128)S(1)}, f32[16,16,256]{2,1,0:T(8,128)}, u32[]{:S(2)}) %copy-start.2) | copy-done | bytes 262168
  3.6 0.0 copy-start.3
  3.6 0.7 %copy-done.3 = s32[16,256]{1,0:T(8,128)S(1)} copy-done((s32[16,256]{1,0:T(8,128)S(1)}, s32[16,256]{1,0:T(8,128)}, u32[]{:S(2)}) %copy-start.3) | copy-done | bytes 16408
  4.3 58.4 %shard_map.91 = f32[16,16,256]{2,1,0:T(8,128)S(1)} custom-call(f32[16,16,256]{2,1,0:T(8,128)S(1)} %copy-done, f32[16,16,256]{2,1,0:T(8,128)S(1)} %copy-done.1, f32[16,16,256]{2,1,0:T(8,128)S(1)} %copy-done.2, s32[16,256]{1,0:T(8,128)S(1)} %copy-done.3, f32[8]{0:T(128)S(1)} %copy-done.4, f32[8]{0:T(128)S(1)} %copy-done.5, s32[1,32]{1,0:T(1,128)S(1)} %bitcast.3, ...), custom_call_target="tpu_custom_call" | custom-call | tf_op jit(solution)/shard_map/pallas_call | solution.py:936
  62.7 0.7 %copy.11 = f32[16,16,256]{2,1,0:T(8,128)} copy(f32[16,16,256]{2,1,0:T(8,128)S(1)} %shard_map.91) | data formatting | bytes 524288
Async XLA Ops:
  0.0 0.7 %copy-start.7 = (f32[1,1,32]{2,1,0:T(1,128)S(1)}, f32[1,1,32]{2,1,0:T(1,128)}, u32[]{:S(2)}) copy-start(f32[1,1,32]{2,1,0:T(1,128)} %param.16) | copy-start | bytes 388
  0.0 0.7 %copy-start.8 = (s32[1,1,32]{2,1,0:T(1,128)S(1)}, s32[1,1,32]{2,1,0:T(1,128)}, u32[]{:S(2)}) copy-start(s32[1,1,32]{2,1,0:T(1,128)} %param.17) | copy-start | bytes 388
  0.0 0.7 %copy-start.4 = (f32[8]{0:T(128)S(1)}, f32[8]{0:T(128)}, u32[]{:S(2)}) copy-start(f32[8]{0:T(128)} %storage_table.1) | copy-start | bytes 100
  0.0 0.7 %copy-start.5 = (f32[8]{0:T(128)S(1)}, f32[8]{0:T(128)}, u32[]{:S(2)}) copy-start(f32[8]{0:T(128)} %return_table.1) | copy-start | bytes 100
  0.0 0.7 %copy-start.6 = (s32[1,1,32]{2,1,0:T(1,128)S(1)}, s32[1,1,32]{2,1,0:T(1,128)}, u32[]{:S(2)}) copy-start(s32[1,1,32]{2,1,0:T(1,128)} %param.15) | copy-start | bytes 388
  0.7 0.9 %copy-start = (f32[16,16,256]{2,1,0:T(8,128)S(1)}, f32[16,16,256]{2,1,0:T(8,128)}, u32[]{:S(2)}) copy-start(f32[16,16,256]{2,1,0:T(8,128)} %residual_in.1) | copy-start | bytes 786436
  1.7 0.9 %copy-start.1 = (f32[16,16,256]{2,1,0:T(8,128)S(1)}, f32[16,16,256]{2,1,0:T(8,128)}, u32[]{:S(2)}) copy-start(f32[16,16,256]{2,1,0:T(8,128)} %pressure_in.1) | copy-start | bytes 786436
  2.6 0.9 %copy-start.2 = (f32[16,16,256]{2,1,0:T(8,128)S(1)}, f32[16,16,256]{2,1,0:T(8,128)}, u32[]{:S(2)}) copy-start(f32[16,16,256]{2,1,0:T(8,128)} %conductivity_in.1) | copy-start | bytes 786436
  3.6 0.7 %copy-start.3 = (s32[16,256]{1,0:T(8,128)S(1)}, s32[16,256]{1,0:T(8,128)}, u32[]{:S(2)}) copy-start(s32[16,256]{1,0:T(8,128)} %land_use_in.1) | copy-start | bytes 49156

commit v4 on v3

--- a/solution.py
+++ b/solution.py
@@ -374,39 +374,67 @@
             value = jnp.where(lane >= 124, rot(south, -4 * (z + 1), 1), 0.0)
             u[z, :, 128:256] = jnp.where(lane < 4, rot(north, -4 * z, 1), value)
 
+    HALF = NZ // 2
+
+    def factor_columns(diag, down, put):
+        top = bottom = None
+        for i in range(HALF):
+            z = i
+            pivot = diag(z) if i == 0 else diag(z) - top * down(z - 1)
+            inverse = 1.0 / pivot
+            top = down(z) * inverse
+            put(z, inverse, top)
+            z = NZ - 1 - i
+            pivot = diag(z) if i == 0 else diag(z) - bottom * down(z)
+            if z == HALF:
+                pivot = pivot - top * down(z - 1)
+            inverse = 1.0 / pivot
+            bottom = down(z - 1) * inverse
+            put(z, inverse, bottom)
+
     def factor(level):
         diag, down, g, inv = (ref[f"{name}{level}"] for name in ("diag", "D", "g", "inv"))
-        before = None
-        for z in range(NZ):
-            pivot = diag[z]
-            if z > 0:
-                pivot = pivot - before * down[z - 1]
-            inverse = 1.0 / pivot
+
+        def put(z, inverse, inwards):
             inv[z] = inverse
-            if z < NZ - 1:
-                before = down[z] * inverse
-                g[z] = before
-
-    def back_substitute(level, update):
-        g, inv, f = (ref[f"{name}{level}"] for name in ("g", "inv", "f"))
-        value = f[NZ - 1] * inv[NZ - 1]
-        update(NZ - 1, value)
-        for z in range(NZ - 2, -1, -1):
-            value = f[z] * inv[z] + g[z] * value
-            update(z, value)
+            g[z] = inwards
+
+        factor_columns(lambda z: diag[z], lambda z: down[z], put)
+
+    def solve_columns(right, g, inv, put_f, get_f, update):
+        top = bottom = None
+        for i in range(HALF):
+            z = i
+            top = right(z) if i == 0 else right(z) + g(z - 1) * top
+            put_f(z, top)
+            z = NZ - 1 - i
+            bottom = right(z) if i == 0 else right(z) + g(z + 1) * bottom
+            if z > HALF:
+                put_f(z, bottom)
+        below = (bottom + g(HALF - 1) * top) * inv(HALF)
+        update(HALF, below)
+        above = below
+        for i in range(HALF):
+            z = HALF - 1 - i
+            above = get_f(z) * inv(z) + g(z) * above
+            update(z, above)
+            z = HALF + 1 + i
+            if z < NZ:
+                below = get_f(z) * inv(z) + g(z) * below
+                update(z, below)
 
     def first_sweep(level):
-        g, f, rhs, u = (ref[f"{name}{level}"] for name in ("g", "f", "rhs", "u"))
-        value = rhs[0]
-        f[0] = value
-        for z in range(1, NZ):
-            value = rhs[z] + g[z - 1] * value
+        g, inv, f, rhs, u = (ref[f"{name}{level}"] for name in ("g", "inv", "f", "rhs", "u"))
+
+        def put_f(z, value):
             f[z] = value
 
         def update(z, solved):
             u[z] = OMEGA * solved
 
-        back_substitute(level, update)
+        solve_columns(
+            lambda z: rhs[z], lambda z: g[z], lambda z: inv[z], put_f, lambda z: f[z], update
+        )
 
     def lateral(level, z, u):
         east, north = ref[f"E{level}"][z], ref[f"N{level}"][z]
@@ -419,20 +447,22 @@
         inv = ref[f"inv{level}"]
         rows, lanes = u.shape[1:] if last is None else last.shape[1:]
         at = (slice(0, rows), slice(0, lanes))
-        value = None
-        for z in range(NZ):
-            right = rhs[(z, *at)] + lateral(level, z, u[z])[at]
-            value = right if z == 0 else right + g[(z - 1, *at)] * value
+
+        def put_f(z, value):
             f[(z, *at)] = value
-        for z in range(NZ - 1, -1, -1):
-            solved = f[(z, *at)] * inv[(z, *at)]
-            value = solved if z == NZ - 1 else solved + g[(z, *at)] * value
+
+        def update(z, solved):
             old = u[(z, *at)]
-            value_new = old + OMEGA * (value - old)
+            value = old + OMEGA * (solved - old)
             if last is None:
-                u[z] = value_new
+                u[z] = value
             else:
-                last[z] = value_new
+                last[z] = value
+
+        solve_columns(
+            lambda z: rhs[(z, *at)] + lateral(level, z, u[z])[at], lambda z: g[(z, *at)],
+            lambda z: inv[(z, *at)], put_f, lambda z: f[(z, *at)], update,
+        )
 
     def remainder(level, z):
         diag, down, rhs, u = (ref[f"{name}{level}"] for name in ("diag", "D", "rhs", "u"))
@@ -486,34 +516,35 @@
     def keep_own(value, fill):
         return jnp.where((row8 < 4) & (lane8 < 64), value, fill)
 
+    def aggregate(level, rows, pieces_of, get):
+        for z in range(NZ):
+            put_rows(ref["ta"], rows, z, get(z))
+        pieces = []
+        for piece in pieces_of:
+            summed = jnp.concatenate(
+                [row_half(ref["ta"], rows, piece, z, 0) + row_half(ref["ta"], rows, piece, z, 1) for z in range(NZ)],
+                axis=0,
+            )
+            pieces.append(layers_of(exact_dot(summed, lane_matrix(piece, "sum")), coarse_rows(rows)))
+        return pieces
+
     def restrict(level):
-        for z in range(NZ):
-            put_rows(ref["ta"], ROWS[level], z, remainder(level, z)[:, 0 : lanes_of(level)])
+        lanes = lanes_of(level)
+        return aggregate(level, ROWS[level], PIECES[level], lambda z: remainder(level, z)[:, 0:lanes])
+
+    def coarsen(level, extra=None):
+        rows_fine = ROWS[level]
+        lanes = lanes_of(level)
+        names = ("E", "N", "D", "diag")
+        buffers = [ref[name] for name in ("ta", "tb", "tc", "td")]
+        for z in range(NZ):
+            for name, buffer in zip(names, buffers):
+                value = ref[f"{name}{level}"][z, 0:rows_fine, 0:lanes]
+                if extra is not None and name == "diag":
+                    value = value + extra[z]
+                put_rows(buffer, rows_fine, z, value)
         pieces = []
         for piece in PIECES[level]:
-            summed = jnp.concatenate(
-                [
-                    row_half(ref["ta"], ROWS[level], piece, z, 0) + row_half(ref["ta"], ROWS[level], piece, z, 1)
-                    for z in range(NZ)
-                ],
-                axis=0,
-            )
-            pieces.append(layers_of(exact_dot(summed, lane_matrix(piece, "sum")), coarse_rows(ROWS[level])))
-        return pieces
-
-    def coarsen(level, own=False):
-        rows_fine = 16 if own else ROWS[level]
-        lanes = 256 if own else lanes_of(level)
-        names = ("E", "N", "D", "diag")
-        buffers = [ref[name] for name in ("ta", "tb", "tc", "td")]
-        for z in range(NZ):
-            for name, buffer in zip(names, buffers):
-                value = ref[f"{name}{level}"][z, 0:rows_fine, 0:lanes]
-                if own and name == "diag":
-                    value = value + ref["S0"][z, 0:rows_fine, 0:lanes]
-                put_rows(buffer, rows_fine, z, value)
-        pieces = []
-        for piece in PIECES[level][0:1] if own else PIECES[level]:
             odd_e, sum_n, sum_d, sum_g = [], [], [], []
             for z in range(NZ):
                 (e0, e1), (n0, n1), (d0, d1), (g0, g1) = (
@@ -674,6 +705,9 @@
         for k in range(1, GX):
             value = value + jnp.where(at_sum, buffer[0, 8 * k : 8 * k + 8, :], 0.0)
         return total_of(value)
+
+    def put_layer(name, z, value):
+        ref[name][16 * z : 16 * z + 16, :] = value
 
     def coarse_at(name, z):
         return ref[name][16 * z : 16 * z + 16, :]
@@ -772,11 +806,9 @@
 
     names = ("E", "N", "D", "diag")
     fills = (0.0, 0.0, 0.0, 1.0)
-    (own1,) = coarsen(0, own=True)
-    for k, name in enumerate(names):
-        for z in range(NZ):
-            ref[f"{name}1"][z, 0:8, 0:128] = own1[k][z]
-    (coarse2,) = coarsen(1)
+    place(1, names, coarsen(0))
+    (own_storage,) = aggregate(0, 16, PIECES[0][0:1], lambda z: ref["S0"][z, 0:16, 0:256])
+    (coarse2,) = coarsen(1, extra=own_storage)
     own2 = [[keep_own(coarse2[k][z], fills[k]) for z in range(NZ)] for k in range(4)]
     pack_wide("c2", lambda k, z: own2[k][z])
     tiles = [pack_tile(value) for value in coarsest_coefficients(coarse2)]
@@ -790,7 +822,13 @@
     for z in range(NZ):
         ref["diag0"][z] = ref["diag0"][z] + ref["S0"][z]
     factor(0)
-    place(1, names, coarsen(0))
+    storage1 = aggregate(0, 32, PIECES[0], lambda z: ref["S0"][z])
+    lane = iota((16, 128), 1)
+    for z in range(NZ):
+        diagonal = ref["diag1"]
+        diagonal[z, :, 0:128] = diagonal[z, :, 0:128] + storage1[0][z]
+        tail = jnp.where((lane < 32) | (lane >= 96), storage1[1][z], 0.0)
+        diagonal[z, :, 128:256] = diagonal[z, :, 128:256] + tail
     factor(1)
 
     receive_columns(copies_r, ref["rhs0"], 2, 0.0)
@@ -831,13 +869,13 @@
 
     prepare23()
     receive_wide("x2", copies_x2, [ref["rhs2"]], (0.0,), False)
-    stage_c = gather_along_x("gc", stage, B_GCX)
     down23()
     (values,) = restrict(3)
     tile = pack_tile(stack_layers(values))
-    stage = gather_columns("gr", [tile], total_of(tile), B_GR1)
+    stage_r = gather_columns("gr", [tile], total_of(tile), B_GR1)
+    stage_c = gather_along_x("gc", stage, B_GCX)
     receive_u1(copies_v1)
-    stage_r = gather_rows("gr", stage, B_GR2)
+    stage_r = gather_rows("gr", stage_r, B_GR2)
     receive_wide("c2", copies_far, two, fills, True)
     receive_wide("x2", copies_far_x, [ref["rhs2"]], (0.0,), True)
     prepare23()
@@ -852,19 +890,19 @@
     lane = iota((16, 128), 1)
     row = iota((16, 128), 0)
     gap = (lane & 63) >= 48
-    before = None
+
+    def put_coarse(z, inverse, inwards):
+        put_layer("inv4", z, inverse)
+        put_layer("g4", z, inwards)
+
+    factor_columns(
+        lambda z: jnp.where(gap, 1.0, coarse_layer(ref["gc_r2"], 0, z)),
+        lambda z: coarse_layer(ref["gc_r2"], 3, z),
+        put_coarse,
+    )
     for z in range(NZ):
-        pivot = jnp.where(gap, 1.0, coarse_layer(ref["gc_r2"], 0, z))
-        if z > 0:
-            pivot = pivot - before * below
-        inverse = 1.0 / pivot
-        below = coarse_layer(ref["gc_r2"], 3, z)
-        before = below * inverse
-        at = slice(16 * z, 16 * z + 16)
-        ref["inv4"][at, :] = inverse
-        ref["g4"][at, :] = before
-        ref["E4"][at, :] = coarse_layer(ref["gc_r2"], 1, z)
-        ref["N4"][at, :] = coarse_layer(ref["gc_r2"], 2, z)
+        put_layer("E4", z, coarse_layer(ref["gc_r2"], 1, z))
+        put_layer("N4", z, coarse_layer(ref["gc_r2"], 2, z))
     storage_total = coarse_sum(ref["gc_r2"])
     for copy in stage_r:
         copy.wait_recv()
@@ -875,21 +913,24 @@
         ref["u4"][at, :] = jnp.broadcast_to(shift, (16, 128))
 
     def coarse_sweep(step, carry):
-        value = None
-        for z in range(NZ):
+        def right(z):
             u, east, north = coarse_at("u4", z), coarse_at("E4", z), coarse_at("N4", z)
             from_e = rot(u, -1, 0)
             from_e = jnp.where(row == 15, rot(from_e, 64, 1), from_e)
             from_w = rot(east * u, 1, 0)
             from_w = jnp.where(row == 0, rot(from_w, 64, 1), from_w)
-            right = coarse_at("rhs4", z) + east * from_e + from_w + north * rot(u, -1, 1) + rot(north * u, 1, 1)
-            value = right if z == 0 else right + coarse_at("g4", z - 1) * value
-            ref["f4"][16 * z : 16 * z + 16, :] = value
-        for z in range(NZ - 1, -1, -1):
-            solved = coarse_at("f4", z) * coarse_at("inv4", z)
-            value = solved if z == NZ - 1 else solved + coarse_at("g4", z) * value
+            return (
+                coarse_at("rhs4", z) + east * from_e + from_w + north * rot(u, -1, 1) + rot(north * u, 1, 1)
+            )
+
+        def update(z, solved):
             old = coarse_at("u4", z)
-            ref["u4"][16 * z : 16 * z + 16, :] = old + OMEGA * (value - old)
+            put_layer("u4", z, old + OMEGA * (solved - old))
+
+        solve_columns(
+            right, lambda z: coarse_at("g4", z), lambda z: coarse_at("inv4", z),
+            lambda z, value: put_layer("f4", z, value), lambda z: coarse_at("f4", z), update,
+        )
         return carry
 
     lax.fori_loop(0, COARSE_SWEEPS, coarse_sweep, 0)
@@ -930,7 +971,7 @@
     well_cells, well_rates, return_cells,
 ):
     vmem = pl.BlockSpec(memory_space=pltpu.VMEM)
-    hbm = pl.BlockSpec(memory_space=pltpu.HBM)
+    hbm = pl.BlockSpec(memory_space=pl.ANY)
     smem = pl.BlockSpec(memory_space=pltpu.SMEM)
     wells = well_cells.shape[-1]
     return pl.pallas_call(
@@ -940,7 +981,7 @@
         out_specs=vmem,
         scratch_shapes=list(PLAN.values()),
         compiler_params=pltpu.CompilerParams(
-            collective_id=0, has_side_effects=True, vmem_limit_bytes=36 * 1024 * 1024
+            collective_id=0, has_side_effects=True, vmem_limit_bytes=54784 * 1024
         ),
     )(
         newton_residual, pressure_head, conductivity, land_use, storage_table, return_table,

time: 64.3 us -> 57.8 us (0.90); the launches traced: 63.4 us -> 57.7 us
  Pallas kernels: 58.4 us -> 55.5 us
  local copies, waits for them, and re-layouts: 4.97 us -> 2.12 us
    pallas_call x1, Pallas kernels: 58.4 us -> 55.5 us  [shards(): pl.pallas_call(kernel, out_shape=jax.ShapeDtypeStruct(newton_residual.sha...]
    unnamed x19 -> x13, local copies, waits for them, and re-layouts: 4.97 us -> 2.12 us
where the time goes in v4:
time: 57.8 us; the launch traced here: 57.7 us
  Pallas kernels  55.5 us (96%)
  local copies, waits for them, and re-layouts  2.12 us (4%)
    pallas_call x1, Pallas kernels, shards(): pl.pallas_call(kernel, out_shape=jax.ShapeDtypeStruct(newton_residual.sha...  55.5 us
    unnamed x13, local copies, waits for them, and re-layouts  2.12 us

profile of v4, /device:TPU:1, one launch (start us, length us, event | category | flops | bytes accessed | tf_op | source)
XLA Modules:
  0.0 57.7 jit_solution(9547948850876463525)
XLA Ops:
  0.0 0.0 copy-start.4
  0.0 0.0 copy-start.5
  0.0 0.0 copy-start.1
  0.0 0.0 copy-start.2
  0.0 0.0 copy-start.3
  0.0 0.6 %copy-done.4 = f32[1,1,32]{2,1,0:T(1,128)S(1)} copy-done((f32[1,1,32]{2,1,0:T(1,128)S(1)}, f32[1,1,32]{2,1,0:T(1,128)}, u32[]{:S(2)}) %copy-start.4) | copy-done | bytes 152
  0.7 0.0 copy-done.5
  0.7 0.0 copy-done.1
  0.7 0.0 copy-done.2
  0.7 0.0 copy-done.3
  0.7 0.0 copy-start
  0.7 0.7 %copy-done = s32[16,256]{1,0:T(8,128)S(1)} copy-done((s32[16,256]{1,0:T(8,128)S(1)}, s32[16,256]{1,0:T(8,128)}, u32[]{:S(2)}) %copy-start) | copy-done | bytes 16408
  1.4 55.5 %shard_map.91 = f32[16,16,256]{2,1,0:T(8,128)S(1)} custom-call(f32[16,16,256]{2,1,0:T(8,128)} %residual_in.1, f32[16,16,256]{2,1,0:T(8,128)} %pressure_in.1, f32[16,16,256]{2,1,0:T(8,128)} %conductivity_in.1, s32[16,256]{1,0:T(8,128)S(1)} %copy-done, f32[8]{0:T(128)S(1)} %copy-done.1, f32[8]{0:T(128)S(1)} %copy-done.2, s32[1,32]{1,0:T(1,128)S(1)} %bitcast.3, ...), custom_call_target="tpu_custom_call" | custom-call | tf_op jit(solution)/shard_map/pallas_call | solution.py:977
  57.0 0.7 %copy.11 = f32[16,16,256]{2,1,0:T(8,128)} copy(f32[16,16,256]{2,1,0:T(8,128)S(1)} %shard_map.91) | data formatting | bytes 524288
Async XLA Ops:
  0.0 0.7 %copy-start.4 = (f32[1,1,32]{2,1,0:T(1,128)S(1)}, f32[1,1,32]{2,1,0:T(1,128)}, u32[]{:S(2)}) copy-start(f32[1,1,32]{2,1,0:T(1,128)} %param.16) | copy-start | bytes 388
  0.0 0.7 %copy-start.5 = (s32[1,1,32]{2,1,0:T(1,128)S(1)}, s32[1,1,32]{2,1,0:T(1,128)}, u32[]{:S(2)}) copy-start(s32[1,1,32]{2,1,0:T(1,128)} %param.17) | copy-start | bytes 388
  0.0 0.7 %copy-start.1 = (f32[8]{0:T(128)S(1)}, f32[8]{0:T(128)}, u32[]{:S(2)}) copy-start(f32[8]{0:T(128)} %storage_table.1) | copy-start | bytes 100
  0.0 0.7 %copy-start.2 = (f32[8]{0:T(128)S(1)}, f32[8]{0:T(128)}, u32[]{:S(2)}) copy-start(f32[8]{0:T(128)} %return_table.1) | copy-start | bytes 100
  0.0 0.7 %copy-start.3 = (s32[1,1,32]{2,1,0:T(1,128)S(1)}, s32[1,1,32]{2,1,0:T(1,128)}, u32[]{:S(2)}) copy-start(s32[1,1,32]{2,1,0:T(1,128)} %param.15) | copy-start | bytes 388
  0.7 0.7 %copy-start = (s32[16,256]{1,0:T(8,128)S(1)}, s32[16,256]{1,0:T(8,128)}, u32[]{:S(2)}) copy-start(s32[16,256]{1,0:T(8,128)} %land_use_in.1) | copy-start | bytes 49156

commit v5 on v4

--- a/solution.py
+++ b/solution.py
@@ -54,8 +54,18 @@
     return (index >= start) & (index < start + count)
 
 
-def exact_dot(left, right):
+def full_dot(left, right):
     return jnp.dot(left, right, precision=lax.Precision.HIGHEST, preferred_element_type=F32)
+
+
+def exact_dot(left, choice):
+    choice = choice.astype(jnp.bfloat16)
+    high = left.astype(jnp.bfloat16)
+    rest = left - high.astype(F32)
+    middle = rest.astype(jnp.bfloat16)
+    low = (rest - middle.astype(F32)).astype(jnp.bfloat16)
+    parts = [jnp.dot(part, choice, preferred_element_type=F32) for part in (high, middle, low)]
+    return parts[0] + (parts[1] + parts[2])
 
 
 def scratch_plan():
@@ -617,11 +627,11 @@
         last_lane = jnp.where(hit & ((fine & 3) == 3), 1.0, 0.0).astype(F32)
         summed = exact_dot(
             jnp.concatenate(
-                [exact_dot(last_row, east), exact_dot(rows, down), exact_dot(rows, diagonal - inner)], axis=0
+                [full_dot(last_row, east), full_dot(rows, down), full_dot(rows, diagonal - inner)], axis=0
             ),
             lanes,
         )
-        north = exact_dot(rows, north)
+        north = full_dot(rows, north)
         north4 = exact_dot(north, last_lane)
         diagonal4 = summed[32:48] - 2.0 * exact_dot(north, lanes - last_lane)
         return diagonal4, summed[0:16], north4, summed[16:32]
@@ -904,6 +914,8 @@
         put_layer("E4", z, coarse_layer(ref["gc_r2"], 1, z))
         put_layer("N4", z, coarse_layer(ref["gc_r2"], 2, z))
     storage_total = coarse_sum(ref["gc_r2"])
+    for copy in started:
+        copy.wait_send()
     for copy in stage_r:
         copy.wait_recv()
     shift = coarse_sum(ref["gr_r2"]) / storage_total
@@ -962,8 +974,6 @@
     prolong(0, lambda i, z: ref["u1"][z, :, 128 * i : 128 * (i + 1)])
     sweep(0)
     sweep(0, last=out)
-    for copy in started:
-        copy.wait_send()
 
 
 def shards(

time: 57.8 us -> 56.4 us (0.976)
  Pallas kernels: 55.5 us -> 53.8 us
    pallas_call x1, Pallas kernels: 55.5 us -> 53.8 us  [shards(): pl.pallas_call(kernel, out_shape=jax.ShapeDtypeStruct(newton_residual.sha...]
where the time goes in v5:
time: 56.4 us; the launch traced here: 56 us
  Pallas kernels  53.8 us (95%)
  local copies, waits for them, and re-layouts  2.12 us (4%)
    pallas_call x1, Pallas kernels, shards(): pl.pallas_call(kernel, out_shape=jax.ShapeDtypeStruct(newton_residual.sha...  53.8 us
    unnamed x13, local copies, waits for them, and re-layouts  2.12 us

profile of v5, /device:TPU:1, one launch (start us, length us, event | category | flops | bytes accessed | tf_op | source)
XLA Modules:
  0.0 56.0 jit_solution(16785295636257738452)
XLA Ops:
  0.0 0.0 copy-start.4
  0.0 0.0 copy-start.5
  0.0 0.0 copy-start.1
  0.0 0.0 copy-start.2
  0.0 0.0 copy-start.3
  0.0 0.6 %copy-done.4 = f32[1,1,32]{2,1,0:T(1,128)S(1)} copy-done((f32[1,1,32]{2,1,0:T(1,128)S(1)}, f32[1,1,32]{2,1,0:T(1,128)}, u32[]{:S(2)}) %copy-start.4) | copy-done | bytes 152
  0.7 0.0 copy-done.5
  0.7 0.0 copy-done.1
  0.7 0.0 copy-done.2
  0.7 0.0 copy-done.3
  0.7 0.0 copy-start
  0.7 0.7 %copy-done = s32[16,256]{1,0:T(8,128)S(1)} copy-done((s32[16,256]{1,0:T(8,128)S(1)}, s32[16,256]{1,0:T(8,128)}, u32[]{:S(2)}) %copy-start) | copy-done | bytes 16408
  1.4 53.8 %shard_map.91 = f32[16,16,256]{2,1,0:T(8,128)S(1)} custom-call(f32[16,16,256]{2,1,0:T(8,128)} %residual_in.1, f32[16,16,256]{2,1,0:T(8,128)} %pressure_in.1, f32[16,16,256]{2,1,0:T(8,128)} %conductivity_in.1, s32[16,256]{1,0:T(8,128)S(1)} %copy-done, f32[8]{0:T(128)S(1)} %copy-done.1, f32[8]{0:T(128)S(1)} %copy-done.2, s32[1,32]{1,0:T(1,128)S(1)} %bitcast.3, ...), custom_call_target="tpu_custom_call" | custom-call | tf_op jit(solution)/shard_map/pallas_call | solution.py:987
  55.3 0.7 %copy.11 = f32[16,16,256]{2,1,0:T(8,128)} copy(f32[16,16,256]{2,1,0:T(8,128)S(1)} %shard_map.91) | data formatting | bytes 524288
Async XLA Ops:
  0.0 0.7 %copy-start.4 = (f32[1,1,32]{2,1,0:T(1,128)S(1)}, f32[1,1,32]{2,1,0:T(1,128)}, u32[]{:S(2)}) copy-start(f32[1,1,32]{2,1,0:T(1,128)} %param.16) | copy-start | bytes 388
  0.0 0.7 %copy-start.5 = (s32[1,1,32]{2,1,0:T(1,128)S(1)}, s32[1,1,32]{2,1,0:T(1,128)}, u32[]{:S(2)}) copy-start(s32[1,1,32]{2,1,0:T(1,128)} %param.17) | copy-start | bytes 388
  0.0 0.7 %copy-start.1 = (f32[8]{0:T(128)S(1)}, f32[8]{0:T(128)}, u32[]{:S(2)}) copy-start(f32[8]{0:T(128)} %storage_table.1) | copy-start | bytes 100
  0.0 0.7 %copy-start.2 = (f32[8]{0:T(128)S(1)}, f32[8]{0:T(128)}, u32[]{:S(2)}) copy-start(f32[8]{0:T(128)} %return_table.1) | copy-start | bytes 100
  0.0 0.7 %copy-start.3 = (s32[1,1,32]{2,1,0:T(1,128)S(1)}, s32[1,1,32]{2,1,0:T(1,128)}, u32[]{:S(2)}) copy-start(s32[1,1,32]{2,1,0:T(1,128)} %param.15) | copy-start | bytes 388
  0.7 0.7 %copy-start = (s32[16,256]{1,0:T(8,128)S(1)}, s32[16,256]{1,0:T(8,128)}, u32[]{:S(2)}) copy-start(s32[16,256]{1,0:T(8,128)} %land_use_in.1) | copy-start | bytes 49156
